TPU v7x, 256 devices: a whole 4x4x8 slice. The times are simulated.
256 devices in a mesh: gx: 4 (over x_hi, core), gy: 8 (over z), gz: 8 (over y, x_lo).
Axes of the slice: x: 4 (x_hi: 2, x_lo: 2; x = x_hi * 2 + x_lo), y: 4, z: 8, core: 2. Of those that a mesh axis runs over, the one named last changes fastest.
Arguments:
- sdf: float32 [64, 512, 1024], P('gx', 'gy', 'gz'), may hold values from -6 to 6
- albedo: float32 [64, 512, 1024], P('gx', 'gy', 'gz'), may hold values from 0.25 to 1
- intensity: float32 [64, 512, 1024], P('gx', 'gy', 'gz'), may hold values from -6 to 6
- direction: float32 [64, 512, 1024], P('gx', 'gy', 'gz'), may hold values from -6 to 6
- lighting: float32 [9], replicated, may hold values from -4 to 4
Outputs:
- gradient: float32 [64, 512, 1024], P('gx', 'gy', 'gz')
- hess_vec: float32 [64, 512, 1024], P('gx', 'gy', 'gz')
- light_grad: float32 [9], replicated
All inputs are finite; a program needn't handle non-finite values.
Results may differ from a plain program's by a relative error of at most 0.00015.
Values sent between devices are 32-bit elements; how exact they have to be, the bound alone decides.
No kernel may reach another device: no remote copies, remote signals or barrier semaphores. Data moves between devices by JAX's collectives and lax.ppermute only.
A program may use at most 128 MiB of HBM per device.

v0:
```python
import jax
import jax.numpy as jnp
from jax import lax
from jax.sharding import PartitionSpec as P

soften = 0.25
reg_weight = 0.02
sh_zero = 0.282095
sh_one = 0.488603
sh_two = 1.092548
sh_three = 0.315392
sh_four = 0.546274


def with_halo(value, sides, width):
    for axis, dim in sides:
        count, length = (lax.axis_size(axis), value.shape[dim])
        up = [(i, (i + 1) % count) for i in range(count - 1)]
        down = [(j, i) for i, j in up]
        last = lax.slice_in_dim(value, length - width, length, axis=dim)
        leading = lax.slice_in_dim(value, 0, width, axis=dim)
        before = lax.ppermute(last, axis, up)
        after = lax.ppermute(leading, axis, down)
        value = jnp.concatenate([before, value, after], axis=dim)
    return value


def central(field):
    return (
        (field[..., 2:, 1:-1, 1:-1] - field[..., :-2, 1:-1, 1:-1]) * 0.5,
        (field[..., 1:-1, 2:, 1:-1] - field[..., 1:-1, :-2, 1:-1]) * 0.5,
        (field[..., 1:-1, 1:-1, 2:] - field[..., 1:-1, 1:-1, :-2]) * 0.5,
    )


def laplace(field):
    return (
        field[..., 2:, 1:-1, 1:-1]
        + field[..., :-2, 1:-1, 1:-1]
        + field[..., 1:-1, 2:, 1:-1]
        + field[..., 1:-1, :-2, 1:-1]
        + field[..., 1:-1, 1:-1, 2:]
        + field[..., 1:-1, 1:-1, :-2]
        - 6.0 * field[..., 1:-1, 1:-1, 1:-1]
    )


def diverge(fx, fy, fz):
    return (
        fx[..., 2:, 1:-1, 1:-1]
        - fx[..., :-2, 1:-1, 1:-1]
        + (fy[..., 1:-1, 2:, 1:-1] - fy[..., 1:-1, :-2, 1:-1])
        + (fz[..., 1:-1, 1:-1, 2:] - fz[..., 1:-1, 1:-1, :-2])
    ) * 0.5


def shading(grads, lighting, albedo, intensity):
    scale = jnp.sqrt(grads[0] * grads[0] + grads[1] * grads[1] + grads[2] * grads[2] + soften)
    nrm_x = grads[0] / scale
    nrm_y = grads[1] / scale
    nrm_z = grads[2] / scale
    basis = [
        jnp.full_like(nrm_x, sh_zero),
        sh_one * nrm_y,
        sh_one * nrm_z,
        sh_one * nrm_x,
        sh_two * nrm_x * nrm_y,
        sh_two * nrm_y * nrm_z,
        sh_three * (3.0 * nrm_z * nrm_z - 1.0),
        sh_two * nrm_x * nrm_z,
        sh_four * (nrm_x * nrm_x - nrm_y * nrm_y),
    ]
    shade = basis[0] * lighting[0]
    for index in range(1, 9):
        shade = shade + lighting[index] * basis[index]
    res = albedo * shade - intensity
    part_x = (
        sh_one * lighting[3]
        + sh_two * (lighting[4] * nrm_y + lighting[7] * nrm_z)
        + 2.0 * sh_four * lighting[8] * nrm_x
    )
    part_y = (
        sh_one * lighting[1]
        + sh_two * (lighting[4] * nrm_x + lighting[5] * nrm_z)
        - 2.0 * sh_four * lighting[8] * nrm_y
    )
    part_z = (
        sh_one * lighting[2]
        + sh_two * (lighting[5] * nrm_y + lighting[7] * nrm_x)
        + 6.0 * sh_three * lighting[6] * nrm_z
    )
    along = nrm_x * part_x + nrm_y * part_y + nrm_z * part_z
    factor = albedo / scale
    jac = (
        (part_x - nrm_x * along) * factor,
        (part_y - nrm_y * along) * factor,
        (part_z - nrm_z * along) * factor,
    )
    return (res, jac, basis)


def totals_of(res, lap_d, albedo, basis, count):
    energy_part = 0.5 * jnp.sum(res * res) + 0.5 * reg_weight * jnp.sum(lap_d * lap_d)
    light_part = jnp.stack([jnp.sum(albedo * term * res) for term in basis])
    energy, light_grad = lax.psum((energy_part, light_part), ("gx", "gy", "gz"))
    return (energy / count, light_grad)


def body(sdf, albedo, intensity, direction, lighting):
    count = (
        float(sdf.shape[0] * lax.axis_size("gx"))
        * float(sdf.shape[1] * lax.axis_size("gy"))
        * float(sdf.shape[2] * lax.axis_size("gz"))
    )
    padded_d, padded_v = (
        with_halo(sdf, (("gx", 0), ("gy", 1), ("gz", 2)), 1),
        with_halo(direction, (("gx", 0), ("gy", 1), ("gz", 2)), 1),
    )
    res, jac, basis = shading(central(padded_d), lighting, albedo, intensity)
    grad_v = central(padded_v)
    lin = jac[0] * grad_v[0] + jac[1] * grad_v[1] + jac[2] * grad_v[2]
    lap_d = laplace(padded_d)
    lap_v = laplace(padded_v)
    damping, light_grad = totals_of(res, lap_d, albedo, basis, count)
    stacked = jnp.stack(
        [
            res * jac[0],
            res * jac[1],
            res * jac[2],
            lin * jac[0],
            lin * jac[1],
            lin * jac[2],
            lap_d,
            lap_v,
        ]
    )
    wide = with_halo(stacked, (("gx", 1), ("gy", 2), ("gz", 3)), 1)
    gradient = -diverge(wide[0], wide[1], wide[2]) + reg_weight * laplace(wide[6])
    hess_vec = (
        -diverge(wide[3], wide[4], wide[5]) + reg_weight * laplace(wide[7]) + damping * direction
    )
    return (gradient, hess_vec, light_grad)


def solution(mesh):
    in_specs = (
        P("gx", "gy", "gz"),
        P("gx", "gy", "gz"),
        P("gx", "gy", "gz"),
        P("gx", "gy", "gz"),
        P(),
    )
    out_specs = (P("gx", "gy", "gz"), P("gx", "gy", "gz"), P())
    return jax.shard_map(body, mesh=mesh, in_specs=in_specs, out_specs=out_specs, check_vma=False)
```

profile of v0, /device:TPU:1, one launch (start us, length us, event | category | flops | bytes accessed | tf_op | source)
XLA Modules:
  0.0 243.1 jit_solution(10599096072346853079)
XLA Ops:
  1.4 5.1 %collective-permute-start.1 = (f32[1,64,128]{2,1,0:T(8,128)S(1)}, f32[1,64,128]{2,1,0:T(8,128)S(1)}, u32[]{:S(2)}, u32[]{:S(2)}) collective-permute-start(f32[1,64,128]{2,1,0:T(8,128)S(1)} %get-tuple-element.57), channel_id=1, source_target_pairs={{64,0},{128,64},{192,128},{65,1},{129,65},{193,129},{66,2},{130,66... | collective-permute-start | bytes 98312 | tf_op jit(solution)/shard_map/ppermute | solution.py:23
  6.6 2.8 %collective-permute-start = (f32[1,64,128]{2,1,0:T(8,128)S(1)}, f32[1,64,128]{2,1,0:T(8,128)S(1)}, u32[]{:S(2)}, u32[]{:S(2)}) collective-permute-start(f32[1,64,128]{2,1,0:T(8,128)S(1)} %get-tuple-element.58), channel_id=1, source_target_pairs={{0,64},{64,128},{128,192},{1,65},{65,129},{129,193},{2,66},{66,130... | collective-permute-start | bytes 98312 | tf_op jit(solution)/shard_map/ppermute | solution.py:22
  10.2 1.9 collective-permute-start.6
  12.1 5.1 %collective-permute-start.7 = (f32[1,64,128]{2,1,0:T(8,128)S(1)}, f32[1,64,128]{2,1,0:T(8,128)S(1)}, u32[]{:S(2)}, u32[]{:S(2)}) collective-permute-start(f32[1,64,128]{2,1,0:T(8,128)S(1)} %get-tuple-element.56), channel_id=1, source_target_pairs={{0,64},{64,128},{128,192},{1,65},{65,129},{129,193},{2,66},{66,130... | collective-permute-start | bytes 98312 | tf_op jit(solution)/shard_map/ppermute | solution.py:22
  17.2 1.6 fusion.30
  23.9 1.1 constant_dynamic-update-slice_fusion.1
  25.1 1.3 constant_dynamic-update-slice_fusion.4
  26.3 1.3 collective-permute-start.2
  27.6 4.2 %collective-permute-start.3 = (f32[18,1,128]{2,1,0:T(1,128)S(1)}, f32[18,1,128]{2,1,0:T(1,128)S(1)}, u32[]{:S(2)}, u32[]{:S(2)}) collective-permute-start(f32[18,1,128]{2,1,0:T(1,128)S(1)} %get-tuple-element.54), channel_id=1, source_target_pairs={{0,8},{8,16},{16,24},{24,32},{32,40},{40,48},{48,56},{1,9},{9,17},... | collective-permute-start | bytes 27656 | tf_op jit(solution)/shard_map/ppermute | solution.py:22
  31.8 3.5 %collective-permute-start.9 = (f32[18,1,128]{2,1,0:T(1,128)S(1)}, f32[18,1,128]{2,1,0:T(1,128)S(1)}, u32[]{:S(2)}, u32[]{:S(2)}) collective-permute-start(f32[18,1,128]{2,1,0:T(1,128)S(1)} %get-tuple-element.51), channel_id=1, source_target_pairs={{0,8},{8,16},{16,24},{24,32},{32,40},{40,48},{48,56},{1,9},{9,17},... | collective-permute-start | bytes 27656 | tf_op jit(solution)/shard_map/ppermute | solution.py:22
  35.4 1.3 collective-permute-start.8
  37.6 3.1 %collective-permute-start.5 = (f32[18,66,1]{1,2,0:T(1,128)S(1)}, f32[18,66,1]{1,2,0:T(1,128)S(1)}, u32[]{:S(2)}, u32[]{:S(2)}) collective-permute-start(f32[18,66,1]{1,2,0:T(1,128)S(1)} %copy.41), channel_id=1, source_target_pairs={{0,1},{1,2},{2,3},{3,4},{4,5},{5,6},{6,7},{8,9},{9,10},{10,11},{11... | collective-permute-start | bytes 14264 | tf_op jit(solution)/shard_map/ppermute | solution.py:22
  40.7 1.3 collective-permute-start.4
  43.4 4.0 %collective-permute-start.11 = (f32[18,66,1]{1,2,0:T(1,128)S(1)}, f32[18,66,1]{1,2,0:T(1,128)S(1)}, u32[]{:S(2)}, u32[]{:S(2)}) collective-permute-start(f32[18,66,1]{1,2,0:T(1,128)S(1)} %copy.45), channel_id=1, source_target_pairs={{0,1},{1,2},{2,3},{3,4},{4,5},{5,6},{6,7},{8,9},{9,10},{10,11},{11... | collective-permute-start | bytes 14264 | tf_op jit(solution)/shard_map/ppermute | solution.py:22
  47.4 1.3 collective-permute-start.10
  49.1 1.2 copy.42
  50.3 6.3 %multiply_reduce_fusion = (f32[]{:T(128)}, f32[]{:T(128)}, f32[]{:T(128)}, f32[]{:T(128)}, f32[]{:T(128)}, /*index=5*/f32[]{:T(128)}, f32[]{:T(128)}, f32[]{:T(1...) fusion(f32[16,64,128]{2,1,0:T(8,128)S(1)} %copy-done.1, ...), kind=kLoop, calls=%fused_computation.75 | loop fusion | flops 11534326 | bytes 4877676 | tf_op jit(solution)/shard_map/reduce_sum | solution.py:104
  56.6 3.3 %bitcast_dynamic-update-slice_fusion.7 = (f32[8,16,64,128]{3,2,1,0:T(8,128)}, f32[16,64,128]{2,1,0:T(8,128)}) fusion(f32[16,64,128]{2,1,0:T(8,128)S(1)} %get-tuple-element.20, f32[16,64,128]{2,1,0:T(8,128)S(1)} %copy-done.1, f32[16,64,128]{2,1,0:T(8,128)S(1)} %get-tuple-element.24, f32[16,64,128]{2,1,0:T(8,128)S(1)} %get-tuple-element.23, ...), kind=kLoop, calls=%fused_computation.74 | loop fusion | flops 4063231 | bytes 4194336
  59.9 3.4 %bitcast_dynamic-update-slice_fusion.6 = (f32[8,16,64,128]{3,2,1,0:T(8,128)}, f32[16,64,128]{2,1,0:T(8,128)}) fusion(f32[8,16,64,128]{3,2,1,0:T(8,128)} %get-tuple-element.31, f32[16,64,128]{2,1,0:T(8,128)S(1)} %get-tuple-element.20, f32[16,64,128]{2,1,0:T(8,128)S(1)} %copy-done.1, f32[16,64,128]{2,1,0:T(8,128)S(1)} %get-tuple-element.24, ...), kind=kLoop, calls=%fused_computation.73 | loop fusion | flops 4063232 | bytes 4198400
  63.3 3.3 %bitcast_dynamic-update-slice_fusion.5 = (f32[8,16,64,128]{3,2,1,0:T(8,128)}, f32[16,64,128]{2,1,0:T(8,128)}) fusion(f32[8,16,64,128]{3,2,1,0:T(8,128)} %get-tuple-element.29, f32[16,64,128]{2,1,0:T(8,128)S(1)} %get-tuple-element.20, f32[16,64,128]{2,1,0:T(8,128)S(1)} %copy-done.1, f32[16,64,128]{2,1,0:T(8,128)S(1)} %get-tuple-element.24, ...), kind=kLoop, calls=%fused_computation.72 | loop fusion | flops 4063232 | bytes 4198400
  66.6 1.0 copy.44
  68.0 3.6 %bitcast_dynamic-update-slice_fusion.4 = (f32[8,16,64,128]{3,2,1,0:T(8,128)}, f32[16,64,128]{2,1,0:T(8,128)S(1)}) fusion(f32[8,16,64,128]{3,2,1,0:T(8,128)} %get-tuple-element.27, f32[16,64,128]{2,1,0:T(8,128)} %get-tuple-element.32, f32[16,64,128]{2,1,0:T(8,128)} %get-tuple-element.28, f32[18,1,128]{2,1,0:T(1,128)S(1)} %collective-permute-done.8, ...), kind=kLoop, calls=%fused_computation.71 | loop fusion | flops 2883584 | bytes 3829024
  71.6 2.0 bitcast_dynamic-update-slice_fusion.3
  74.5 1.2 multiply_reduce_fusion.9
  76.6 1.3 bitcast_dynamic-update-slice_fusion
  78.0 1.1 fusion.23
  79.0 4.0 %collective-permute-start.12 = (f32[8,1,64,128]{3,2,1,0:T(8,128)S(1)}, f32[8,1,64,128]{3,2,1,0:T(8,128)S(1)}, u32[]{:S(2)}, u32[]{:S(2)}) collective-permute-start(f32[8,1,64,128]{3,2,1,0:T(8,128)S(1)} %get-tuple-element.45), channel_id=1, source_target_pairs={{0,64},{64,128},{128,192},{1,65},{65,129},{129,193},{2,66},{66,130... | collective-permute-start | bytes 786440 | tf_op jit(solution)/shard_map/ppermute | solution.py:22
  83.1 1.9 collective-permute-start.13
  85.0 1.4 collective-permute-done.12
  86.4 5.9 %collective-permute-done.13 = f32[8,1,64,128]{3,2,1,0:T(8,128)S(1)} collective-permute-done((f32[8,1,64,128]{3,2,1,0:T(8,128)S(1)}, f32[8,1,64,128]{3,2,1,0:T(8,128)S(1)}, u32[]{:S(2)}, u32[]{:S(2)}) %collective-permute-start.13) | collective-permute-done | bytes 262176 | tf_op jit(solution)/shard_map/ppermute | solution.py:23
  92.3 1.3 pad_maximum_fusion.26
  93.6 1.3 collective-permute-start.15
  94.9 4.9 %collective-permute-start.14 = (f32[8,18,1,128]{3,0,2,1:T(8,128)S(1)}, f32[8,18,1,128]{3,0,2,1:T(8,128)S(1)}, u32[]{:S(2)}, u32[]{:S(2)}) collective-permute-start(f32[8,18,1,128]{3,0,2,1:T(8,128)S(1)} %copy.47), channel_id=1, source_target_pairs={{0,8},{8,16},{16,24},{24,32},{32,40},{40,48},{48,56},{1,9},{9,17},... | collective-permute-start | bytes 221192 | tf_op jit(solution)/shard_map/ppermute | solution.py:22
  99.9 1.3 collective-permute-done.14
  101.3 2.7 %pad_maximum_fusion.1 = f32[8,18,66,128]{3,2,1,0:T(8,128)S(1)} fusion(f32[8,18,1,128]{3,2,1,0:T(1,128)S(1)} %copy.50, f32[8,1,64,128]{3,2,1,0:T(8,128)S(1)} %collective-permute-done.13, f32[8,16,64,128]{3,2,1,0:T(8,128)} %bitcast_dynamic-update-slice_fusion, f32[8,1,64,128]{3,2,1,0:T(8,128)S(1)} %collective-permute-done.12, f32[8,18,1,128]{3,2,1,0:T(1,128)S(1)} %copy.49), kind=kLoop, calls=%fused_computation.1 | loop fusion | flops 4866048 | bytes 9732096 | tf_op jit(solution)/shard_map/concatenate | solution.py:24
  104.0 5.7 %fusion.22 = (f32[8,18,66,1]{3,2,1,0:T(8,128)}, f32[8,18,66,1]{3,2,1,0:T(8,128)}) fusion(f32[8,18,66,128]{3,2,1,0:T(8,128)S(1)} %pad_maximum_fusion.1), kind=kLoop, calls=%fused_computation.119 | loop fusion | bytes 152064 | tf_op jit(solution)/shard_map/slice | solution.py:20
  109.7 3.5 %copy.51 = f32[8,18,66,1]{2,0,3,1:T(8,128)S(1)} copy(f32[8,18,66,1]{3,2,1,0:T(8,128)} %get-tuple-element.41) | data formatting | bytes 76032 | tf_op jit(solution)/shard_map/slice | solution.py:20
  113.2 3.7 %collective-permute-start.16 = (f32[8,18,66,1]{2,0,3,1:T(8,128)S(1)}, f32[8,18,66,1]{2,0,3,1:T(8,128)S(1)}, u32[]{:S(2)}, u32[]{:S(2)}) collective-permute-start(f32[8,18,66,1]{2,0,3,1:T(8,128)S(1)} %copy.51), channel_id=1, source_target_pairs={{0,1},{1,2},{2,3},{3,4},{4,5},{5,6},{6,7},{8,9},{9,10},{10,11},{11... | collective-permute-start | bytes 114056 | tf_op jit(solution)/shard_map/ppermute | solution.py:22
  116.9 3.5 %copy.52 = f32[8,18,66,1]{2,0,3,1:T(8,128)S(1)} copy(f32[8,18,66,1]{3,2,1,0:T(8,128)} %get-tuple-element.42) | data formatting | bytes 76032 | tf_op jit(solution)/shard_map/slice | solution.py:21
  120.5 1.3 collective-permute-start.17
  123.1 5.7 %stack.75 = f32[9]{0:T(128)S(1)} concatenate(f32[1]{0:T(128)} %bitcast.27, f32[1]{0:T(128)} %bitcast.28, f32[1]{0:T(128)} %bitcast.29, f32[1]{0:T(128)} %bitcast.30, f32[1]{0:T(128)} %bitcast.31, f32[1]{0:T(128)} %bitcast.32, f32[1]{0:T(128)} %bitcast.33, f32[1]{0:T(128)} %bitcast.34, f32[1]{0:T(128)} %bitcast.35), dimensions={0} | concatenate | bytes 72 | tf_op jit(solution)/shard_map/stack | solution.py:104
  128.8 83.2 %all-reduce = (f32[]{:T(128)}, f32[9]{0:T(128)}) all-reduce(f32[]{:T(128)S(6)} %add.214, f32[9]{0:T(128)S(1)} %stack.75), channel_id=1, replica_groups=mesh['gx'=4,'gy'=8,'gz'=8] {'gx','gy','gz'}, use_global_device_ids=true, to_apply=%region_2.0 | all-reduce | flops 10 | bytes 80 | tf_op jit(solution)/shard_map/psum | solution.py:105
  212.7 3.4 %copy.53 = f32[8,18,66,1]{3,2,1,0:T(8,128)} copy(f32[8,18,66,1]{2,0,3,1:T(8,128)S(1)} %collective-permute-done.16) | data formatting | bytes 76032 | tf_op jit(solution)/shard_map/ppermute | solution.py:22
  216.1 3.4 %copy.54 = f32[8,18,66,1]{3,2,1,0:T(8,128)} copy(f32[8,18,66,1]{2,0,3,1:T(8,128)S(1)} %collective-permute-done.17) | data formatting | bytes 76032 | tf_op jit(solution)/shard_map/ppermute | solution.py:23
  219.5 12.6 %pad_maximum_fusion = f32[8,18,66,130]{3,2,1,0:T(8,128)S(1)} fusion(f32[8,18,66,1]{3,2,1,0:T(8,128)} %copy.54, f32[8,18,1,128]{3,2,1,0:T(1,128)S(1)} %copy.50, f32[8,1,64,128]{3,2,1,0:T(8,128)S(1)} %collective-permute-done.13, f32[8,16,64,128]{3,2,1,0:T(8,128)} %bitcast_dynamic-update-slice_fusion, f32[8,1,64,128]{3,2,1,0:T(8,128)S(1)} %collective-permute-done.12, ...), kind=kLoop, calls=%fused_computation | loop fusion | flops 7413120 | bytes 9884160 | tf_op jit(solution)/shard_map/concatenate | solution.py:24
  232.1 3.2 %slice_bitcast_fusion.3 = (f32[18,66,130]{2,1,0:T(8,128)}, f32[18,66,130]{2,1,0:T(8,128)S(1)}, f32[18,66,130]{2,1,0:T(8,128)}, f32[18,66,130]{2,1,0:T(8,128)}, f...) fusion(f32[8,18,66,130]{3,2,1,0:T(8,128)S(1)} %pad_maximum_fusion), kind=kLoop, calls=%fused_computation.5 | loop fusion | bytes 9884160 | tf_op jit(solution)/shard_map/squeeze | solution.py:140
  235.4 5.3 %fusion.11 = f32[16,64,128]{2,1,0:T(8,128)} fusion(f32[18,66,130]{2,1,0:T(8,128)S(1)} %get-tuple-element.37, f32[18,66,130]{2,1,0:T(8,128)} %get-tuple-element.38, f32[18,66,130]{2,1,0:T(8,128)} %get-tuple-element.39, f32[18,66,130]{2,1,0:T(8,128)} %get-tuple-element.40), kind=kLoop, calls=%fused_computation.34 | loop fusion | flops 2097152 | bytes 7340032 | tf_op jit(solution)/shard_map/add | solution.py:138
  240.7 2.4 fusion.4
  (63 shorter events, 6.6 us)
Async XLA Ops:
  1.4 23.6 %collective-permute-start.1 = (f32[1,64,128]{2,1,0:T(8,128)S(1)}, f32[1,64,128]{2,1,0:T(8,128)S(1)}, u32[]{:S(2)}, u32[]{:S(2)}) collective-permute-start(f32[1,64,128]{2,1,0:T(8,128)S(1)} %get-tuple-element.57), channel_id=1, source_target_pairs={{64,0},{128,64},{192,128},{65,1},{129,65},{193,129},{66,2},{130,66... | collective-permute-start | bytes 98312 | tf_op jit(solution)/shard_map/ppermute | solution.py:23
  6.6 17.3 %collective-permute-start = (f32[1,64,128]{2,1,0:T(8,128)S(1)}, f32[1,64,128]{2,1,0:T(8,128)S(1)}, u32[]{:S(2)}, u32[]{:S(2)}) collective-permute-start(f32[1,64,128]{2,1,0:T(8,128)S(1)} %get-tuple-element.58), channel_id=1, source_target_pairs={{0,64},{64,128},{128,192},{1,65},{65,129},{129,193},{2,66},{66,130... | collective-permute-start | bytes 98312 | tf_op jit(solution)/shard_map/ppermute | solution.py:22
  10.2 21.6 %collective-permute-start.6 = (f32[1,64,128]{2,1,0:T(8,128)S(1)}, f32[1,64,128]{2,1,0:T(8,128)S(1)}, u32[]{:S(2)}, u32[]{:S(2)}) collective-permute-start(f32[1,64,128]{2,1,0:T(8,128)S(1)} %get-tuple-element.55), channel_id=1, source_target_pairs={{64,0},{128,64},{192,128},{65,1},{129,65},{193,129},{66,2},{130,66... | collective-permute-start | bytes 98312 | tf_op jit(solution)/shard_map/ppermute | solution.py:23
  12.1 13.0 %collective-permute-start.7 = (f32[1,64,128]{2,1,0:T(8,128)S(1)}, f32[1,64,128]{2,1,0:T(8,128)S(1)}, u32[]{:S(2)}, u32[]{:S(2)}) collective-permute-start(f32[1,64,128]{2,1,0:T(8,128)S(1)} %get-tuple-element.56), channel_id=1, source_target_pairs={{0,64},{64,128},{128,192},{1,65},{65,129},{129,193},{2,66},{66,130... | collective-permute-start | bytes 98312 | tf_op jit(solution)/shard_map/ppermute | solution.py:22
  25.0 25.3 %copy-start.3 = (f32[18,64,128]{2,1,0:T(8,128)}, f32[18,64,128]{2,1,0:T(8,128)S(1)}, u32[]{:S(2)}) copy-start(f32[18,64,128]{2,1,0:T(8,128)S(1)} %constant_dynamic-update-slice_fusion) | copy-start | bytes 1769476
  26.3 10.4 %collective-permute-start.2 = (f32[18,1,128]{2,1,0:T(1,128)S(1)}, f32[18,1,128]{2,1,0:T(1,128)S(1)}, u32[]{:S(2)}, u32[]{:S(2)}) collective-permute-start(f32[18,1,128]{2,1,0:T(1,128)S(1)} %get-tuple-element.53), channel_id=1, source_target_pairs={{8,0},{16,8},{24,16},{32,24},{40,32},{48,40},{56,48},{9,1},{17,9},... | collective-permute-start | bytes 27656 | tf_op jit(solution)/shard_map/ppermute | solution.py:23
  27.6 9.1 %collective-permute-start.3 = (f32[18,1,128]{2,1,0:T(1,128)S(1)}, f32[18,1,128]{2,1,0:T(1,128)S(1)}, u32[]{:S(2)}, u32[]{:S(2)}) collective-permute-start(f32[18,1,128]{2,1,0:T(1,128)S(1)} %get-tuple-element.54), channel_id=1, source_target_pairs={{0,8},{8,16},{16,24},{24,32},{32,40},{40,48},{48,56},{1,9},{9,17},... | collective-permute-start | bytes 27656 | tf_op jit(solution)/shard_map/ppermute | solution.py:22
  31.8 10.5 %copy-start.5 = (f32[18,64,128]{2,1,0:T(8,128)}, f32[18,64,128]{2,1,0:T(8,128)S(1)}, u32[]{:S(2)}) copy-start(f32[18,64,128]{2,1,0:T(8,128)S(1)} %constant_dynamic-update-slice_fusion.3) | copy-start | bytes 1769476
  31.8 10.1 %collective-permute-start.9 = (f32[18,1,128]{2,1,0:T(1,128)S(1)}, f32[18,1,128]{2,1,0:T(1,128)S(1)}, u32[]{:S(2)}, u32[]{:S(2)}) collective-permute-start(f32[18,1,128]{2,1,0:T(1,128)S(1)} %get-tuple-element.51), channel_id=1, source_target_pairs={{0,8},{8,16},{16,24},{24,32},{32,40},{40,48},{48,56},{1,9},{9,17},... | collective-permute-start | bytes 27656 | tf_op jit(solution)/shard_map/ppermute | solution.py:22
  35.4 6.6 %collective-permute-start.8 = (f32[18,1,128]{2,1,0:T(1,128)S(1)}, f32[18,1,128]{2,1,0:T(1,128)S(1)}, u32[]{:S(2)}, u32[]{:S(2)}) collective-permute-start(f32[18,1,128]{2,1,0:T(1,128)S(1)} %get-tuple-element.52), channel_id=1, source_target_pairs={{8,0},{16,8},{24,16},{32,24},{40,32},{48,40},{56,48},{9,1},{17,9},... | collective-permute-start | bytes 27656 | tf_op jit(solution)/shard_map/ppermute | solution.py:23
  37.0 13.2 %copy-start.1 = (f32[16,64,128]{2,1,0:T(8,128)S(1)}, f32[16,64,128]{2,1,0:T(8,128)}, u32[]{:S(2)}) copy-start(f32[16,64,128]{2,1,0:T(8,128)} %param.6) | copy-start | bytes 1572868
  37.6 11.5 %collective-permute-start.5 = (f32[18,66,1]{1,2,0:T(1,128)S(1)}, f32[18,66,1]{1,2,0:T(1,128)S(1)}, u32[]{:S(2)}, u32[]{:S(2)}) collective-permute-start(f32[18,66,1]{1,2,0:T(1,128)S(1)} %copy.41), channel_id=1, source_target_pairs={{0,1},{1,2},{2,3},{3,4},{4,5},{5,6},{6,7},{8,9},{9,10},{10,11},{11... | collective-permute-start | bytes 14264 | tf_op jit(solution)/shard_map/ppermute | solution.py:22
  40.7 8.1 %collective-permute-start.4 = (f32[18,66,1]{1,2,0:T(1,128)S(1)}, f32[18,66,1]{1,2,0:T(1,128)S(1)}, u32[]{:S(2)}, u32[]{:S(2)}) collective-permute-start(f32[18,66,1]{1,2,0:T(1,128)S(1)} %copy.39), channel_id=1, source_target_pairs={{1,0},{2,1},{3,2},{4,3},{5,4},{6,5},{7,6},{9,8},{10,9},{11,10},{12... | collective-permute-start | bytes 14264 | tf_op jit(solution)/shard_map/ppermute | solution.py:23
  43.4 24.2 %collective-permute-start.11 = (f32[18,66,1]{1,2,0:T(1,128)S(1)}, f32[18,66,1]{1,2,0:T(1,128)S(1)}, u32[]{:S(2)}, u32[]{:S(2)}) collective-permute-start(f32[18,66,1]{1,2,0:T(1,128)S(1)} %copy.45), channel_id=1, source_target_pairs={{0,1},{1,2},{2,3},{3,4},{4,5},{5,6},{6,7},{8,9},{9,10},{10,11},{11... | collective-permute-start | bytes 14264 | tf_op jit(solution)/shard_map/ppermute | solution.py:22
  47.4 19.2 %collective-permute-start.10 = (f32[18,66,1]{1,2,0:T(1,128)}, f32[18,66,1]{1,2,0:T(1,128)}, u32[]{:S(2)}, u32[]{:S(2)}) collective-permute-start(f32[18,66,1]{1,2,0:T(1,128)} %copy.43), channel_id=1, source_target_pairs={{1,0},{2,1},{3,2},{4,3},{5,4},{6,5},{7,6},{9,8},{10,9},{11,10},{12... | collective-permute-start | bytes 14264 | tf_op jit(solution)/shard_map/ppermute | solution.py:23
  59.9 8.1 %copy-start = (f32[16,64,128]{2,1,0:T(8,128)S(1)}, f32[16,64,128]{2,1,0:T(8,128)}, u32[]{:S(2)}) copy-start(f32[16,64,128]{2,1,0:T(8,128)} %param.8) | copy-start | bytes 1572868
  68.0 5.6 %copy-start.8 = (f32[16,64,128]{2,1,0:T(8,128)S(1)}, f32[16,64,128]{2,1,0:T(8,128)}, u32[]{:S(2)}) copy-start(f32[16,64,128]{2,1,0:T(8,128)} %get-tuple-element.28) | copy-start | bytes 1572868
  68.0 6.5 %copy-start.2 = (f32[18,66,1]{2,1,0:T(8,128)S(1)}, f32[18,66,1]{2,1,0:T(8,128)}, u32[]{:S(2)}) copy-start(f32[18,66,1]{2,1,0:T(8,128)} %copy.42) | copy-start | bytes 14260
  68.0 6.5 %copy-start.4 = (f32[18,64,128]{2,1,0:T(8,128)S(1)}, f32[18,64,128]{2,1,0:T(8,128)}, u32[]{:S(2)}) copy-start(f32[18,64,128]{2,1,0:T(8,128)} %copy-done.3) | copy-start | bytes 1769476
  68.0 6.5 %copy-start.7 = (f32[16,64,128]{2,1,0:T(8,128)S(1)}, f32[16,64,128]{2,1,0:T(8,128)}, u32[]{:S(2)}) copy-start(f32[16,64,128]{2,1,0:T(8,128)} %param.5) | copy-start | bytes 1572868
  71.6 5.0 %copy-start.6 = (f32[18,64,128]{2,1,0:T(8,128)S(1)}, f32[18,64,128]{2,1,0:T(8,128)}, u32[]{:S(2)}) copy-start(f32[18,64,128]{2,1,0:T(8,128)} %copy-done.5) | copy-start | bytes 1769476
  79.0 7.3 %collective-permute-start.12 = (f32[8,1,64,128]{3,2,1,0:T(8,128)S(1)}, f32[8,1,64,128]{3,2,1,0:T(8,128)S(1)}, u32[]{:S(2)}, u32[]{:S(2)}) collective-permute-start(f32[8,1,64,128]{3,2,1,0:T(8,128)S(1)} %get-tuple-element.45), channel_id=1, source_target_pairs={{0,64},{64,128},{128,192},{1,65},{65,129},{129,193},{2,66},{66,130... | collective-permute-start | bytes 786440 | tf_op jit(solution)/shard_map/ppermute | solution.py:22
  83.1 9.2 %collective-permute-start.13 = (f32[8,1,64,128]{3,2,1,0:T(8,128)S(1)}, f32[8,1,64,128]{3,2,1,0:T(8,128)S(1)}, u32[]{:S(2)}, u32[]{:S(2)}) collective-permute-start(f32[8,1,64,128]{3,2,1,0:T(8,128)S(1)} %get-tuple-element.46), channel_id=1, source_target_pairs={{64,0},{128,64},{192,128},{65,1},{129,65},{193,129},{66,2},{130,66... | collective-permute-start | bytes 786440 | tf_op jit(solution)/shard_map/ppermute | solution.py:23
  93.6 6.2 %collective-permute-start.15 = (f32[8,18,1,128]{3,0,2,1:T(8,128)S(1)}, f32[8,18,1,128]{3,0,2,1:T(8,128)S(1)}, u32[]{:S(2)}, u32[]{:S(2)}) collective-permute-start(f32[8,18,1,128]{3,0,2,1:T(8,128)S(1)} %copy.48), channel_id=1, source_target_pairs={{8,0},{16,8},{24,16},{32,24},{40,32},{48,40},{56,48},{9,1},{17,9},... | collective-permute-start | bytes 221192 | tf_op jit(solution)/shard_map/ppermute | solution.py:23
  94.9 6.3 %collective-permute-start.14 = (f32[8,18,1,128]{3,0,2,1:T(8,128)S(1)}, f32[8,18,1,128]{3,0,2,1:T(8,128)S(1)}, u32[]{:S(2)}, u32[]{:S(2)}) collective-permute-start(f32[8,18,1,128]{3,0,2,1:T(8,128)S(1)} %copy.47), channel_id=1, source_target_pairs={{0,8},{8,16},{16,24},{24,32},{32,40},{40,48},{48,56},{1,9},{9,17},... | collective-permute-start | bytes 221192 | tf_op jit(solution)/shard_map/ppermute | solution.py:22
  113.2 99.5 %collective-permute-start.16 = (f32[8,18,66,1]{2,0,3,1:T(8,128)S(1)}, f32[8,18,66,1]{2,0,3,1:T(8,128)S(1)}, u32[]{:S(2)}, u32[]{:S(2)}) collective-permute-start(f32[8,18,66,1]{2,0,3,1:T(8,128)S(1)} %copy.51), channel_id=1, source_target_pairs={{0,1},{1,2},{2,3},{3,4},{4,5},{5,6},{6,7},{8,9},{9,10},{10,11},{11... | collective-permute-start | bytes 114056 | tf_op jit(solution)/shard_map/ppermute | solution.py:22
  120.5 95.6 %collective-permute-start.17 = (f32[8,18,66,1]{2,0,3,1:T(8,128)S(1)}, f32[8,18,66,1]{2,0,3,1:T(8,128)S(1)}, u32[]{:S(2)}, u32[]{:S(2)}) collective-permute-start(f32[8,18,66,1]{2,0,3,1:T(8,128)S(1)} %copy.52), channel_id=1, source_target_pairs={{1,0},{2,1},{3,2},{4,3},{5,4},{6,5},{7,6},{9,8},{10,9},{11,10},{12... | collective-permute-start | bytes 114056 | tf_op jit(solution)/shard_map/ppermute | solution.py:23
  235.4 5.3 %copy-start.9 = (f32[18,66,130]{2,1,0:T(8,128)S(1)}, f32[18,66,130]{2,1,0:T(8,128)}, u32[]{:S(2)}) copy-start(f32[18,66,130]{2,1,0:T(8,128)} %get-tuple-element.33) | copy-start | bytes 1853284
  235.4 5.3 %copy-start.10 = (f32[18,66,130]{2,1,0:T(8,128)S(1)}, f32[18,66,130]{2,1,0:T(8,128)}, u32[]{:S(2)}) copy-start(f32[18,66,130]{2,1,0:T(8,128)} %get-tuple-element.35) | copy-start | bytes 1853284
  235.4 5.3 %copy-start.11 = (f32[18,66,130]{2,1,0:T(8,128)S(1)}, f32[18,66,130]{2,1,0:T(8,128)}, u32[]{:S(2)}) copy-start(f32[18,66,130]{2,1,0:T(8,128)} %get-tuple-element.36) | copy-start | bytes 1853284
where the time goes:
time: 244 us; the launch traced here: 243 us
  blocking collectives  83.2 us (34%)
  starting transfers between devices  52 us (21%)
  other arithmetic  49.8 us (20%)
  local copies, waits for them, and re-layouts  41.4 us (17%)
  waiting for transfers between devices  8.6 us (4%)
  between operations  8.05 us (3%)
    psum x1, blocking collectives, totals_of(): energy, light_grad = lax.psum((energy_part, light_part), ('gx', 'gy', 'gz'))  83.2 us
    ppermute x9, starting transfers between devices, with_halo(): before = lax.ppermute(last, axis, up)  35.3 us
    ppermute x9, starting transfers between devices, with_halo(): after = lax.ppermute(leading, axis, down)  16.7 us
    unnamed x6, other arithmetic  16.5 us
    concatenate x4, other arithmetic, with_halo(): value = jnp.concatenate([before, value, after], axis=dim)  15.4 us
    slice x7, local copies, waits for them, and re-layouts, with_halo(): last = lax.slice_in_dim(value, length - width, length, axis=dim)  10.9 us
    slice x9, local copies, waits for them, and re-layouts, with_halo(): leading = lax.slice_in_dim(value, 0, width, axis=dim)  6.75 us
    reduce_sum x1, other arithmetic, totals_of(): light_part = jnp.stack([jnp.sum(albedo * term * res) for term in basis])  6.31 us
  transfers between devices with their start and end apart: 18, of which 3 were waited for; matrix products, arithmetic and copies ran while one was open for 16% of the time, Pallas kernels for 0%

commit v1 on v0

v1 whole, which is shorter than its diff:
```python
import jax
import jax.numpy as jnp
from jax import lax
from jax.experimental import pallas as pl
from jax.experimental.pallas import tpu as pltpu
from jax.sharding import PartitionSpec as P

reg_weight = 0.02
sh_zero = 0.282095
sh_one = 0.488603
sh_two = 1.092548
sh_three = 0.315392
sh_four = 0.546274

AXES = ("gx", "gy", "gz")
LANES = 128
ROWS = 8
PAD = 8
PARAMS = pltpu.CompilerParams(vmem_limit_bytes=40 * 1024 * 1024)


def lane_ids(rows):
    return lax.broadcasted_iota(jnp.int32, (rows, LANES), 1)


def fold(tall, width):
    parts = LANES // width
    rows = tall.shape[0] // parts
    lanes = lane_ids(rows)
    out = tall[:rows]
    for g in range(1, parts):
        moved = pltpu.roll(tall[g * rows : (g + 1) * rows], g * width, 1)
        out = jnp.where((lanes >= g * width) & (lanes < (g + 1) * width), moved, out)
    return out


def unfold(packed, width):
    parts = LANES // width
    pieces = [packed] + [pltpu.roll(packed, LANES - g * width, 1) for g in range(1, parts)]
    return jnp.concatenate(pieces, axis=0)


def edge_flags():
    flags = []
    for axis in AXES:
        index, count = lax.axis_index(axis), lax.axis_size(axis)
        flags.append(
            (
                jnp.where(index > 0, 1.0, 0.0).astype(jnp.float32),
                jnp.where(index < count - 1, 1.0, 0.0).astype(jnp.float32),
            )
        )
    return flags


def pack_kernel(d_ref, v_ref, xu, xd, yu, yd, zu, zd):
    nx, ny, nz = d_ref.shape
    lanes = lane_ids(ny)
    up = jnp.zeros((ny, LANES), jnp.float32)
    down = jnp.zeros((ny, LANES), jnp.float32)
    for f, ref in enumerate((d_ref, v_ref)):
        xu[f] = ref[nx - 1]
        xd[f] = ref[0]
        for x in range(nx):
            yu[f, x : x + 1, :] = ref[x, ny - 1 : ny, :]
            yd[f, x : x + 1, :] = ref[x, 0:1, :]
            lane = f * nx + x
            plane = ref[x]
            up = jnp.where(lanes == lane, pltpu.roll(plane, lane + 1, 1), up)
            moved = plane if lane == 0 else pltpu.roll(plane, lane, 1)
            down = jnp.where(lanes == lane, moved, down)
    zu[...] = fold(up, 2 * nx)
    zd[...] = fold(down, 2 * nx)


def main_kernel(
    light, d_ref, a_ref, i_ref, v_ref, xp, xn, yp, yn, zp, zn,
    gp, hp, mxu, mxd, myu, myd, mzu, mzd, sums,
    dpad, vpad, zprev, znext, cent, ay, by, bx, ax, zup, zdn, accs,
):
    nx, ny, nz = d_ref.shape
    (fxp, fxn), (fyp, fyn), (fzp, fzn) = edge_flags()
    for f, (ref, pad) in enumerate(((d_ref, dpad), (v_ref, vpad))):
        pad[1 : nx + 1, PAD : PAD + ny, :] = ref[...]
        pad[0, PAD : PAD + ny, :] = xp[f] * fxp
        pad[nx + 1, PAD : PAD + ny, :] = xn[f] * fxn
        before = yp[f] * fyp
        after = yn[f] * fyn
        for x in range(nx):
            pad[x + 1, PAD - 1 : PAD, :] = before[x : x + 1]
            pad[x + 1, PAD + ny : PAD + ny + 1, :] = after[x : x + 1]
    zprev[...] = unfold(zp[...] * fzp, 2 * nx)
    znext[...] = unfold(zn[...] * fzn, 2 * nx)
    zero_row = jnp.zeros((1, LANES), jnp.float32)
    for u in range(2):
        ay[u, PAD + ny : PAD + ny + 1, :] = zero_row
        by[u, PAD - 1 : PAD, :] = zero_row
    zero = jnp.zeros((ROWS, LANES), jnp.float32)
    zup[...] = jnp.zeros((ny, LANES), jnp.float32)
    zdn[...] = jnp.zeros((ny, LANES), jnp.float32)
    bx[...] = jnp.zeros(bx.shape, jnp.float32)
    gp[0] = jnp.zeros((ny, LANES), jnp.float32)
    hp[0] = jnp.zeros((ny, LANES), jnp.float32)
    for k in range(accs.shape[0]):
        accs[k] = zero

    l = [light[k] for k in range(9)]
    c1, c2, c3 = sh_one * l[1], sh_one * l[2], sh_one * l[3]
    c4, c5, c7 = sh_two * l[4], sh_two * l[5], sh_two * l[7]
    c6, c8 = 6.0 * sh_three * l[6], 2.0 * sh_four * l[8]
    base = sh_zero * l[0] - sh_three * l[6]
    lanes = lane_ids(ROWS)
    first, final = lanes == 0, lanes == LANES - 1

    def shifted(pad, f, x, at, mid):
        xm = pad[x, at : at + ROWS, :]
        xq = pad[x + 2, at : at + ROWS, :]
        ym = pad[x + 1, at - 1 : at - 1 + ROWS, :]
        yq = pad[x + 1, at + 1 : at + 1 + ROWS, :]
        lane = f * nx + x
        rows = slice(at - PAD, at - PAD + ROWS)
        halo_m = pltpu.roll(zprev[rows, :], (LANES - lane) & (LANES - 1), 1)
        halo_q = pltpu.roll(znext[rows, :], LANES - 1 - lane, 1)
        zm = jnp.where(first, halo_m, pltpu.roll(mid, 1, 1))
        zq = jnp.where(final, halo_q, pltpu.roll(mid, LANES - 1, 1))
        lap = (xm + xq) + (ym + yq) + (zm + zq) - 6.0 * mid
        return xq - xm, yq - ym, zq - zm, lap

    def plane(x, _):
        for c in range(ny // ROWS):
            at = PAD + c * ROWS
            rows = slice(c * ROWS, (c + 1) * ROWS)
            mid = dpad[x + 1, at : at + ROWS, :]
            hx, hy, hz, lap = shifted(dpad, 0, x, at, mid)
            inv = lax.rsqrt(hx * hx + hy * hy + hz * hz + 1.0)
            nrx, nry, nrz = hx * inv, hy * inv, hz * inv
            px = c3 + c4 * nry + c7 * nrz + c8 * nrx
            py = c1 + c4 * nrx + c5 * nrz - c8 * nry
            pz = c2 + c5 * nry + c7 * nrx + c6 * nrz
            along = nrx * px + nry * py + nrz * pz
            linear = c1 * nry + c2 * nrz + c3 * nrx
            shade = base + 0.5 * (along + linear)
            albedo = a_ref[x, rows, :]
            res = albedo * shade - i_ref[x, rows, :]
            qx, qy, qz = px - nrx * along, py - nry * along, pz - nrz * along
            scale = albedo * inv
            w = albedo * res
            wx, wy, wz = w * nrx, w * nry, w * nrz
            terms = (
                w, wy, wz, wx, wx * nry, wy * nrz, wz * nrz, wx * nrz,
                wx * nrx - wy * nry, res * res + reg_weight * (lap * lap),
            )
            for k, term in enumerate(terms):
                accs[k] = accs[k] + term
            vmid = vpad[x + 1, at : at + ROWS, :]
            ux, uy, uz, vlap = shifted(vpad, 1, x, at, vmid)
            lin = scale * (qx * ux + qy * uy + qz * uz)
            for u, (weight, lapl) in enumerate(((res * scale, lap), (lin * scale, vlap))):
                reg = reg_weight * lapl
                rx, ry, rz = weight * qx, weight * qy, weight * qz
                ay[u, at : at + ROWS, :] = reg - ry
                by[u, at : at + ROWS, :] = reg + ry
                lane = u * nx + x
                fwd = pltpu.roll(reg + rz, 1, 1)
                bwd = pltpu.roll(reg - rz, LANES - 1, 1)
                zup[rows, :] = jnp.where(lanes == lane, pltpu.roll(fwd, lane, 1), zup[rows, :])
                zdn[rows, :] = jnp.where(lanes == lane, pltpu.roll(bwd, lane + 1, 1), zdn[rows, :])
                out = (gp, hp)[u]
                out[x, rows, :] = out[x, rows, :] + (reg - rx)
                cent[u, rows, :] = (
                    bx[u, rows, :]
                    - 6.0 * reg
                    + jnp.where(first, 0.0, fwd)
                    + jnp.where(final, 0.0, bwd)
                )
                bx[u, rows, :] = reg + rx
        for u in range(2):
            out = (gp, hp)[u]
            for c in range(ny // ROWS):
                at = PAD + c * ROWS
                rows = slice(c * ROWS, (c + 1) * ROWS)
                out[x + 1, rows, :] = (
                    cent[u, rows, :]
                    + ay[u, at + 1 : at + 1 + ROWS, :]
                    + by[u, at - 1 : at - 1 + ROWS, :]
                )
            myd[u, pl.ds(x, 1), :] = ay[u, PAD : PAD + 1, :]
            myu[u, pl.ds(x, 1), :] = by[u, PAD + ny - 1 : PAD + ny, :]
        return 0

    lax.fori_loop(0, nx, plane, 0)
    for u in range(2):
        mxu[u] = bx[u]
        mxd[u] = (gp, hp)[u][0]
    mzu[...] = fold(zup[...], 2 * nx)
    mzd[...] = fold(zdn[...], 2 * nx)
    line = lax.broadcasted_iota(jnp.int32, (1, LANES), 1)
    row = jnp.zeros((1, LANES), jnp.float32)
    for k in range(accs.shape[0]):
        row = jnp.where(line == k, jnp.sum(accs[k]), row)
    sums[...] = jnp.broadcast_to(row, sums.shape)


def final_kernel(count, all_sums, v_ref, gp, hp, xp, xn, yp, yn, zp, zn, g_ref, h_ref, t_ref, zprev, znext):
    nx, ny, nz = v_ref.shape
    (fxp, fxn), (fyp, fyn), (fzp, fzn) = edge_flags()
    row = jnp.sum(all_sums[...], axis=0, keepdims=True)
    line = lax.broadcasted_iota(jnp.int32, (1, LANES), 1)
    damping = jnp.sum(jnp.where(line == 9, row, 0.0)) * (0.5 / count)
    weight = jnp.where(line == 0, sh_zero, 0.0)
    for k, factor in enumerate((sh_one, sh_one, sh_one, sh_two, sh_two, 3.0 * sh_three, sh_two, sh_four)):
        weight = jnp.where(line == k + 1, factor, weight)
    shift = jnp.sum(jnp.where(line == 0, row, 0.0)) * sh_three
    t_ref[...] = row * weight - jnp.where(line == 6, shift, 0.0)
    zprev[...] = unfold(zp[...] * fzp, 2 * nx)
    znext[...] = unfold(zn[...] * fzn, 2 * nx)
    lanes = lane_ids(ny)
    first, final = lanes == 0, lanes == LANES - 1
    for u, (ref, out) in enumerate(((gp, g_ref), (hp, h_ref))):
        before = yp[u] * fyp
        after = yn[u] * fyn
        for x in range(nx):
            lane = u * nx + x
            value = ref[x + 1]
            value = value + jnp.where(first, pltpu.roll(zprev[...], (LANES - lane) % LANES, 1), 0.0)
            value = value + jnp.where(final, pltpu.roll(znext[...], LANES - 1 - lane, 1), 0.0)
            if u == 1:
                value = value + damping * v_ref[x]
            if x == 0:
                value = value + xp[u] * fxp
            if x == nx - 1:
                value = value + xn[u] * fxn
            out[x] = value
            out[x, 0:1, :] = out[x, 0:1, :] + before[x : x + 1]
            out[x, ny - 1 : ny, :] = out[x, ny - 1 : ny, :] + after[x : x + 1]


def exchange(ups, downs):
    got = []
    for axis, up, down in zip(AXES, ups, downs):
        count = lax.axis_size(axis)
        forward = [(i, (i + 1) % count) for i in range(count)]
        backward = [(j, i) for i, j in forward]
        got.append(lax.ppermute(up, axis, forward))
        got.append(lax.ppermute(down, axis, backward))
    return got


def body(sdf, albedo, intensity, direction, lighting):
    nx, ny, nz = sdf.shape
    devices = 1
    for axis in AXES:
        devices *= lax.axis_size(axis)
    count = float(nx * ny * nz) * devices
    f32 = lambda *shape: jax.ShapeDtypeStruct(shape, jnp.float32)
    rows = ny * 2 * nx // LANES
    faces = [f32(2, ny, nz)] * 2 + [f32(2, nx, nz)] * 2 + [f32(rows, LANES)] * 2
    vmem = pl.BlockSpec(memory_space=pltpu.VMEM)
    smem = pl.BlockSpec(memory_space=pltpu.SMEM)

    xu, xd, yu, yd, zu, zd = pl.pallas_call(
        pack_kernel, out_shape=faces, in_specs=[vmem] * 2, out_specs=[vmem] * 6, compiler_params=PARAMS
    )(sdf, direction)
    halos = exchange((xu, yu, zu), (xd, yd, zd))
    scratch = lambda *shape: pltpu.VMEM(shape, jnp.float32)
    tall = ny + 2 * PAD
    gp, hp, xu, xd, yu, yd, zu, zd, sums = pl.pallas_call(
        main_kernel,
        out_shape=[f32(nx + 1, ny, nz)] * 2 + faces + [f32(devices, LANES)],
        in_specs=[smem] + [vmem] * 10,
        out_specs=[vmem] * 9,
        scratch_shapes=[
            scratch(nx + 2, tall, nz), scratch(nx + 2, tall, nz),
            scratch(ny, LANES), scratch(ny, LANES),
            scratch(2, ny, nz), scratch(2, tall, nz), scratch(2, tall, nz),
            scratch(2, ny, nz), scratch(2, ny, nz),
            scratch(ny, LANES), scratch(ny, LANES), scratch(10, ROWS, LANES),
        ],
        compiler_params=PARAMS,
    )(lighting, sdf, albedo, intensity, direction, *halos)
    halos = exchange((xu, yu, zu), (xd, yd, zd))
    all_sums = lax.all_to_all(sums, AXES, 0, 0, tiled=True)
    gradient, hess_vec, totals = pl.pallas_call(
        lambda *refs: final_kernel(count, *refs),
        out_shape=[f32(nx, ny, nz)] * 2 + [f32(1, LANES)],
        in_specs=[vmem] * 10,
        out_specs=[vmem] * 3,
        scratch_shapes=[scratch(ny, LANES), scratch(ny, LANES)],
        compiler_params=PARAMS,
    )(all_sums, direction, gp, hp, *halos)
    return gradient, hess_vec, totals[0, :9]


def solution(mesh):
    grid = P("gx", "gy", "gz")
    return jax.shard_map(
        body,
        mesh=mesh,
        in_specs=(grid, grid, grid, grid, P()),
        out_specs=(grid, grid, P()),
        check_vma=False,
    )
```

time: 244 us -> 54.3 us (0.22)
  blocking collectives: 83.2 us -> 0 us
  other arithmetic: 49.8 us -> 0 us
  local copies, waits for them, and re-layouts: 41.4 us -> 2.61 us
  starting transfers between devices: 52 us -> 37.8 us
  Pallas kernels: 0 us -> 9.53 us
  between operations: 8.05 us -> 0.72 us
  waiting for transfers between devices: 8.6 us -> 2.87 us
    psum x1 -> x0, blocking collectives: 83.2 us -> none  [totals_of(): energy, light_grad = lax.psum((energy_part, light_part), ('gx', 'gy', 'gz'))]
    ppermute x18 -> x12, starting transfers between devices: 52 us -> 23.9 us  [the longest x6 12.9 us: exchange(): got.append(lax.ppermute(down, axis, backward))]
    slice x17 -> x0, local copies, waits for them, and re-layouts: 19.3 us -> none  [the longest x7 10.9 us: with_halo(): last = lax.slice_in_dim(value, length - width, length, axis=dim)]
    unnamed x6 -> x0, other arithmetic: 16.5 us -> none
    concatenate x4 -> x0, other arithmetic: 15.4 us -> none  [with_halo(): value = jnp.concatenate([before, value, after], axis=dim)]
    all_to_all x0 -> x1, starting transfers between devices: none -> 13.9 us  [body(): all_sums = lax.all_to_all(sums, AXES, 0, 0, tiled=True)]
    ppermute x8 -> x0, local copies, waits for them, and re-layouts: 9.87 us -> none  [the longest x4 4.98 us: with_halo(): before = lax.ppermute(last, axis, up)]
    pallas_call x0 -> x3, Pallas kernels: none -> 9.53 us  [the longest x1 7.3 us: body(): pl.pallas_call(main_kernel, out_shape=[f32(nx + 1, ny, nz)] * 2 + faces +...]
  transfers between devices with their start and end apart: 18 -> 13, of which waited for: 3 -> 4; matrix products, arithmetic and copies ran while one was open for 16% -> 0% of each run, Pallas kernels for 0% -> 0%
where the time goes in v1:
time: 54.3 us; the launch traced here: 53.5 us
  starting transfers between devices  37.8 us (70%)
  Pallas kernels  9.53 us (18%)
  waiting for transfers between devices  2.87 us (5%)
  local copies, waits for them, and re-layouts  2.61 us (5%)
  between operations  0.72 us (1%)
    all_to_all x1, starting transfers between devices, body(): all_sums = lax.all_to_all(sums, AXES, 0, 0, tiled=True)  13.9 us
    ppermute x6, starting transfers between devices, exchange(): got.append(lax.ppermute(down, axis, backward))  12.9 us
    ppermute x6, starting transfers between devices, exchange(): got.append(lax.ppermute(up, axis, forward))  11 us
    pallas_call x1, Pallas kernels, body(): pl.pallas_call(main_kernel, out_shape=[f32(nx + 1, ny, nz)] * 2 + faces +...  7.3 us
    unnamed x12, local copies, waits for them, and re-layouts  2.1 us
    ppermute x6, waiting for transfers between devices, exchange(): got.append(lax.ppermute(down, axis, backward))  1.6 us
    pallas_call x1, Pallas kernels, body(): pl.pallas_call(lambda *refs: final_kernel(count, *refs), out_shape=[f32(n...  1.57 us
  transfers between devices with their start and end apart: 13, of which 4 were waited for; matrix products, arithmetic and copies ran while one was open for 0% of the time, Pallas kernels for 0%

profile of v1, /device:TPU:1, one launch (start us, length us, event | category | flops | bytes accessed | tf_op | source)
XLA Modules:
  0.0 53.5 jit_solution(9723202544234918732)
XLA Ops:
  0.6 0.0 copy-start
  0.6 1.0 %copy-done = f32[16,64,128]{2,1,0:T(8,128)S(1)} copy-done((f32[16,64,128]{2,1,0:T(8,128)S(1)}, f32[16,64,128]{2,1,0:T(8,128)}, u32[]{:S(2)}) %copy-start) | copy-done | bytes 524312
  1.7 0.0 copy-start.2
  1.7 1.0 %copy-done.2 = f32[16,64,128]{2,1,0:T(8,128)S(1)} copy-done((f32[16,64,128]{2,1,0:T(8,128)S(1)}, f32[16,64,128]{2,1,0:T(8,128)}, u32[]{:S(2)}) %copy-start.2) | copy-done | bytes 524312
  2.7 0.0 copy-start.3
  2.7 0.0 copy-start.4
  2.7 0.7 %shard_map.76 = (f32[2,64,128]{2,1,0:T(8,128)S(1)}, f32[2,64,128]{2,1,0:T(8,128)S(1)}, f32[2,16,128]{2,1,0:T(8,128)S(1)}, f32[2,16,128]{2,1,0:T(8,128)S(1)}, f32...) custom-call(f32[16,64,128]{2,1,0:T(8,128)S(1)} %copy-done.2, f32[16,64,128]{2,1,0:T(8,128)S(1)} %copy-done), custom_call_target="tpu_custom_call" | custom-call | tf_op jit(solution)/shard_map/pallas_call | solution.py:261
  3.4 4.2 %collective-permute-start = (f32[2,64,128]{2,1,0:T(8,128)S(1)}, f32[2,64,128]{2,1,0:T(8,128)S(1)}, u32[]{:S(2)}, u32[]{:S(2)}) collective-permute-start(f32[2,64,128]{2,1,0:T(8,128)S(1)} %get-tuple-element.21), channel_id=1, source_target_pairs={{0,64},{64,128},{128,192},{192,0},{1,65},{65,129},{129,193},{193,1... | collective-permute-start | bytes 196616 | tf_op jit(solution)/shard_map/ppermute | solution.py:244
  7.6 0.0 collective-permute-start.1
  7.6 0.3 collective-permute-start.4
  7.9 1.6 %collective-permute-start.2 = (f32[2,16,128]{2,1,0:T(8,128)S(1)}, f32[2,16,128]{2,1,0:T(8,128)S(1)}, u32[]{:S(2)}, u32[]{:S(2)}) collective-permute-start(f32[2,16,128]{2,1,0:T(8,128)S(1)} %get-tuple-element.23), channel_id=1, source_target_pairs={{0,8},{8,16},{16,24},{24,32},{32,40},{40,48},{48,56},{56,0},{1,9},... | collective-permute-start | bytes 49160 | tf_op jit(solution)/shard_map/ppermute | solution.py:244
  9.5 0.0 copy-start.5
  9.5 3.9 %collective-permute-start.3 = (f32[2,16,128]{2,1,0:T(8,128)S(1)}, f32[2,16,128]{2,1,0:T(8,128)S(1)}, u32[]{:S(2)}, u32[]{:S(2)}) collective-permute-start(f32[2,16,128]{2,1,0:T(8,128)S(1)} %get-tuple-element.24), channel_id=1, source_target_pairs={{8,0},{16,8},{24,16},{32,24},{40,32},{48,40},{56,48},{0,56},{9,1},... | collective-permute-start | bytes 49160 | tf_op jit(solution)/shard_map/ppermute | solution.py:245
  13.5 0.0 collective-permute-done.4.zp
  13.5 3.3 %collective-permute-start.5 = (f32[16,128]{1,0:T(8,128)S(1)}, f32[16,128]{1,0:T(8,128)S(1)}, u32[]{:S(2)}, u32[]{:S(2)}) collective-permute-start(f32[16,128]{1,0:T(8,128)S(1)} %get-tuple-element.26), channel_id=1, source_target_pairs={{1,0},{2,1},{3,2},{4,3},{5,4},{6,5},{7,6},{0,7},{9,8},{10,9},{11,1... | collective-permute-start | bytes 24584 | tf_op jit(solution)/shard_map/ppermute | solution.py:245
  16.8 0.8 %collective-permute-done.5.zn = f32[16,128]{1,0:T(8,128)S(1)} collective-permute-done((f32[16,128]{1,0:T(8,128)S(1)}, f32[16,128]{1,0:T(8,128)S(1)}, u32[]{:S(2)}, u32[]{:S(2)}) %collective-permute-start.5) | collective-permute-done | bytes 8224 | tf_op jit(solution)/shard_map/ppermute | solution.py:245
  17.6 0.0 collective-permute-done.2.yp
  17.6 0.0 collective-permute-done.3.yn
  17.6 0.0 collective-permute-done.xp
  17.6 0.0 collective-permute-done.1.xn
  17.6 0.0 copy-done.3
  17.6 0.0 copy-done.4
  17.6 0.0 copy-done.5
  17.6 0.0 copy-start.1
  17.6 7.3 %shard_map.77 = (f32[17,64,128]{2,1,0:T(8,128)S(1)}, f32[17,64,128]{2,1,0:T(8,128)S(1)}, f32[2,64,128]{2,1,0:T(8,128)S(1)}, f32[2,64,128]{2,1,0:T(8,128)S(1)}, f...) custom-call(f32[9]{0:T(128)S(1)} %copy-done.5, ...), custom_call_target="tpu_custom_call" | custom-call | tf_op jit(solution)/shard_map/pallas_call | solution.py:267
  24.9 13.9 %all-to-all-start = ((f32[256,1,128]{2,1,0:T(1,128)}), f32[256,1,128]{2,1,0:T(1,128)S(1)}, u32[]{:S(2)}, u32[]{:S(2)}) async-start(f32[256,1,128]{2,1,0:T(1,128)} %bitcast.1), calls=%async_computation | async-start | bytes 262144 | tf_op jit(solution)/shard_map/all_to_all | solution.py:282
  38.8 3.2 %collective-permute-start.6 = (f32[2,64,128]{2,1,0:T(8,128)S(1)}, f32[2,64,128]{2,1,0:T(8,128)S(1)}, u32[]{:S(2)}, u32[]{:S(2)}) collective-permute-start(f32[2,64,128]{2,1,0:T(8,128)S(1)} %get-tuple-element.30), channel_id=1, source_target_pairs={{0,64},{64,128},{128,192},{192,0},{1,65},{65,129},{129,193},{193,1... | collective-permute-start | bytes 196616 | tf_op jit(solution)/shard_map/ppermute | solution.py:244
  42.0 0.0 collective-permute-start.7
  42.0 0.3 collective-permute-start.10
  42.3 1.4 %collective-permute-start.8 = (f32[2,16,128]{2,1,0:T(8,128)S(1)}, f32[2,16,128]{2,1,0:T(8,128)S(1)}, u32[]{:S(2)}, u32[]{:S(2)}) collective-permute-start(f32[2,16,128]{2,1,0:T(8,128)S(1)} %get-tuple-element.32), channel_id=1, source_target_pairs={{0,8},{8,16},{16,24},{24,32},{32,40},{40,48},{48,56},{56,0},{1,9},... | collective-permute-start | bytes 49160 | tf_op jit(solution)/shard_map/ppermute | solution.py:244
  43.7 2.8 %collective-permute-start.9 = (f32[2,16,128]{2,1,0:T(8,128)S(1)}, f32[2,16,128]{2,1,0:T(8,128)S(1)}, u32[]{:S(2)}, u32[]{:S(2)}) collective-permute-start(f32[2,16,128]{2,1,0:T(8,128)S(1)} %get-tuple-element.33), channel_id=1, source_target_pairs={{8,0},{16,8},{24,16},{32,24},{40,32},{48,40},{56,48},{0,56},{9,1},... | collective-permute-start | bytes 49160 | tf_op jit(solution)/shard_map/ppermute | solution.py:245
  46.5 0.4 collective-permute-done.10.refs_8_
  47.0 2.8 %collective-permute-start.11 = (f32[16,128]{1,0:T(8,128)S(1)}, f32[16,128]{1,0:T(8,128)S(1)}, u32[]{:S(2)}, u32[]{:S(2)}) collective-permute-start(f32[16,128]{1,0:T(8,128)S(1)} %get-tuple-element.35), channel_id=1, source_target_pairs={{1,0},{2,1},{3,2},{4,3},{5,4},{6,5},{7,6},{0,7},{9,8},{10,9},{11,1... | collective-permute-start | bytes 24584 | tf_op jit(solution)/shard_map/ppermute | solution.py:245
  49.8 0.8 %collective-permute-done.11.refs_9_ = f32[16,128]{1,0:T(8,128)S(1)} collective-permute-done((f32[16,128]{1,0:T(8,128)S(1)}, f32[16,128]{1,0:T(8,128)S(1)}, u32[]{:S(2)}, u32[]{:S(2)}) %collective-permute-start.11) | collective-permute-done | bytes 8224 | tf_op jit(solution)/shard_map/ppermute | solution.py:245
  50.6 0.0 collective-permute-done.8.refs_6_
  50.6 0.0 collective-permute-done.9.refs_7_
  50.6 0.0 collective-permute-done.6.refs_4_
  50.6 0.0 collective-permute-done.7.refs_5_
  50.6 0.8 %all-to-all-done = f32[256,1,128]{2,1,0:T(1,128)S(1)} async-done(((f32[256,1,128]{2,1,0:T(1,128)}), f32[256,1,128]{2,1,0:T(1,128)S(1)}, u32[]{:S(2)}, u32[]{:S(2)}) %all-to-all-start) | async-done | bytes 131104 | tf_op jit(solution)/shard_map/all_to_all | solution.py:282
  51.4 0.0 copy-done.1
  51.4 1.6 %shard_map.78 = (f32[16,64,128]{2,1,0:T(8,128)}, f32[16,64,128]{2,1,0:T(8,128)}, f32[1,128]{1,0:T(1,128)S(1)}) custom-call(f32[256,128]{1,0:T(8,128)S(1)} %bitcast.6, f32[16,64,128]{2,1,0:T(8,128)S(1)} %copy-done.1, f32[17,64,128]{2,1,0:T(8,128)S(1)} %get-tuple-element.28.refs_2_, f32[17,64,128]{2,1,0:T(8,128)S(1)} %get-tuple-element.29.refs_3_, ...), custom_call_target="tpu_custom_call" | custom-call | tf_op jit(solution)/shard_map/pallas_call | solution.py:283
  53.0 0.5 slice_bitcast_fusion
Async XLA Ops:
  0.6 1.0 %copy-start = (f32[16,64,128]{2,1,0:T(8,128)S(1)}, f32[16,64,128]{2,1,0:T(8,128)}, u32[]{:S(2)}) copy-start(f32[16,64,128]{2,1,0:T(8,128)} %refs_1_.1) | copy-start | bytes 1572868
  1.7 1.0 %copy-start.2 = (f32[16,64,128]{2,1,0:T(8,128)S(1)}, f32[16,64,128]{2,1,0:T(8,128)}, u32[]{:S(2)}) copy-start(f32[16,64,128]{2,1,0:T(8,128)} %d_ref.3) | copy-start | bytes 1572868
  2.7 14.9 %copy-start.3 = (f32[16,64,128]{2,1,0:T(8,128)S(1)}, f32[16,64,128]{2,1,0:T(8,128)}, u32[]{:S(2)}) copy-start(f32[16,64,128]{2,1,0:T(8,128)} %a_ref.1) | copy-start | bytes 1572868
  2.7 14.9 %copy-start.4 = (f32[16,64,128]{2,1,0:T(8,128)S(1)}, f32[16,64,128]{2,1,0:T(8,128)}, u32[]{:S(2)}) copy-start(f32[16,64,128]{2,1,0:T(8,128)} %i_ref.1) | copy-start | bytes 1572868
  3.4 14.2 %collective-permute-start = (f32[2,64,128]{2,1,0:T(8,128)S(1)}, f32[2,64,128]{2,1,0:T(8,128)S(1)}, u32[]{:S(2)}, u32[]{:S(2)}) collective-permute-start(f32[2,64,128]{2,1,0:T(8,128)S(1)} %get-tuple-element.21), channel_id=1, source_target_pairs={{0,64},{64,128},{128,192},{192,0},{1,65},{65,129},{129,193},{193,1... | collective-permute-start | bytes 196616 | tf_op jit(solution)/shard_map/ppermute | solution.py:244
  7.6 10.0 %collective-permute-start.1 = (f32[2,64,128]{2,1,0:T(8,128)S(1)}, f32[2,64,128]{2,1,0:T(8,128)S(1)}, u32[]{:S(2)}, u32[]{:S(2)}) collective-permute-start(f32[2,64,128]{2,1,0:T(8,128)S(1)} %get-tuple-element.22), channel_id=1, source_target_pairs={{64,0},{128,64},{192,128},{0,192},{65,1},{129,65},{193,129},{1,193... | collective-permute-start | bytes 196616 | tf_op jit(solution)/shard_map/ppermute | solution.py:245
  7.6 5.9 %collective-permute-start.4 = (f32[16,128]{1,0:T(8,128)S(1)}, f32[16,128]{1,0:T(8,128)S(1)}, u32[]{:S(2)}, u32[]{:S(2)}) collective-permute-start(f32[16,128]{1,0:T(8,128)S(1)} %get-tuple-element.25), channel_id=1, source_target_pairs={{0,1},{1,2},{2,3},{3,4},{4,5},{5,6},{6,7},{7,0},{8,9},{9,10},{10,1... | collective-permute-start | bytes 24584 | tf_op jit(solution)/shard_map/ppermute | solution.py:244
  7.9 9.6 %collective-permute-start.2 = (f32[2,16,128]{2,1,0:T(8,128)S(1)}, f32[2,16,128]{2,1,0:T(8,128)S(1)}, u32[]{:S(2)}, u32[]{:S(2)}) collective-permute-start(f32[2,16,128]{2,1,0:T(8,128)S(1)} %get-tuple-element.23), channel_id=1, source_target_pairs={{0,8},{8,16},{16,24},{24,32},{32,40},{40,48},{48,56},{56,0},{1,9},... | collective-permute-start | bytes 49160 | tf_op jit(solution)/shard_map/ppermute | solution.py:244
  9.5 8.0 %copy-start.5 = (f32[9]{0:T(128)S(1)}, f32[9]{0:T(128)}, u32[]{:S(2)}) copy-start(f32[9]{0:T(128)} %light.1) | copy-start | bytes 112
  9.5 8.0 %collective-permute-start.3 = (f32[2,16,128]{2,1,0:T(8,128)S(1)}, f32[2,16,128]{2,1,0:T(8,128)S(1)}, u32[]{:S(2)}, u32[]{:S(2)}) collective-permute-start(f32[2,16,128]{2,1,0:T(8,128)S(1)} %get-tuple-element.24), channel_id=1, source_target_pairs={{8,0},{16,8},{24,16},{32,24},{40,32},{48,40},{56,48},{0,56},{9,1},... | collective-permute-start | bytes 49160 | tf_op jit(solution)/shard_map/ppermute | solution.py:245
  13.5 4.1 %collective-permute-start.5 = (f32[16,128]{1,0:T(8,128)S(1)}, f32[16,128]{1,0:T(8,128)S(1)}, u32[]{:S(2)}, u32[]{:S(2)}) collective-permute-start(f32[16,128]{1,0:T(8,128)S(1)} %get-tuple-element.26), channel_id=1, source_target_pairs={{1,0},{2,1},{3,2},{4,3},{5,4},{6,5},{7,6},{0,7},{9,8},{10,9},{11,1... | collective-permute-start | bytes 24584 | tf_op jit(solution)/shard_map/ppermute | solution.py:245
  17.6 33.8 %copy-start.1 = (f32[16,64,128]{2,1,0:T(8,128)S(1)}, f32[16,64,128]{2,1,0:T(8,128)}, u32[]{:S(2)}) copy-start(f32[16,64,128]{2,1,0:T(8,128)} %refs_1_.1) | copy-start | bytes 1572868
  24.9 26.5 %all-to-all-start = ((f32[256,1,128]{2,1,0:T(1,128)}), f32[256,1,128]{2,1,0:T(1,128)S(1)}, u32[]{:S(2)}, u32[]{:S(2)}) async-start(f32[256,1,128]{2,1,0:T(1,128)} %bitcast.1), calls=%async_computation | async-start | bytes 262144 | tf_op jit(solution)/shard_map/all_to_all | solution.py:282
  38.8 11.8 %collective-permute-start.6 = (f32[2,64,128]{2,1,0:T(8,128)S(1)}, f32[2,64,128]{2,1,0:T(8,128)S(1)}, u32[]{:S(2)}, u32[]{:S(2)}) collective-permute-start(f32[2,64,128]{2,1,0:T(8,128)S(1)} %get-tuple-element.30), channel_id=1, source_target_pairs={{0,64},{64,128},{128,192},{192,0},{1,65},{65,129},{129,193},{193,1... | collective-permute-start | bytes 196616 | tf_op jit(solution)/shard_map/ppermute | solution.py:244
  42.0 8.6 %collective-permute-start.7 = (f32[2,64,128]{2,1,0:T(8,128)S(1)}, f32[2,64,128]{2,1,0:T(8,128)S(1)}, u32[]{:S(2)}, u32[]{:S(2)}) collective-permute-start(f32[2,64,128]{2,1,0:T(8,128)S(1)} %get-tuple-element.31), channel_id=1, source_target_pairs={{64,0},{128,64},{192,128},{0,192},{65,1},{129,65},{193,129},{1,193... | collective-permute-start | bytes 196616 | tf_op jit(solution)/shard_map/ppermute | solution.py:245
  42.0 4.9 %collective-permute-start.10 = (f32[16,128]{1,0:T(8,128)S(1)}, f32[16,128]{1,0:T(8,128)S(1)}, u32[]{:S(2)}, u32[]{:S(2)}) collective-permute-start(f32[16,128]{1,0:T(8,128)S(1)} %get-tuple-element.34), channel_id=1, source_target_pairs={{0,1},{1,2},{2,3},{3,4},{4,5},{5,6},{6,7},{7,0},{8,9},{9,10},{10,1... | collective-permute-start | bytes 24584 | tf_op jit(solution)/shard_map/ppermute | solution.py:244
  42.3 8.3 %collective-permute-start.8 = (f32[2,16,128]{2,1,0:T(8,128)S(1)}, f32[2,16,128]{2,1,0:T(8,128)S(1)}, u32[]{:S(2)}, u32[]{:S(2)}) collective-permute-start(f32[2,16,128]{2,1,0:T(8,128)S(1)} %get-tuple-element.32), channel_id=1, source_target_pairs={{0,8},{8,16},{16,24},{24,32},{32,40},{40,48},{48,56},{56,0},{1,9},... | collective-permute-start | bytes 49160 | tf_op jit(solution)/shard_map/ppermute | solution.py:244
  43.7 6.9 %collective-permute-start.9 = (f32[2,16,128]{2,1,0:T(8,128)S(1)}, f32[2,16,128]{2,1,0:T(8,128)S(1)}, u32[]{:S(2)}, u32[]{:S(2)}) collective-permute-start(f32[2,16,128]{2,1,0:T(8,128)S(1)} %get-tuple-element.33), channel_id=1, source_target_pairs={{8,0},{16,8},{24,16},{32,24},{40,32},{48,40},{56,48},{0,56},{9,1},... | collective-permute-start | bytes 49160 | tf_op jit(solution)/shard_map/ppermute | solution.py:245
  47.0 3.6 %collective-permute-start.11 = (f32[16,128]{1,0:T(8,128)S(1)}, f32[16,128]{1,0:T(8,128)S(1)}, u32[]{:S(2)}, u32[]{:S(2)}) collective-permute-start(f32[16,128]{1,0:T(8,128)S(1)} %get-tuple-element.35), channel_id=1, source_target_pairs={{1,0},{2,1},{3,2},{4,3},{5,4},{6,5},{7,6},{0,7},{9,8},{10,9},{11,1... | collective-permute-start | bytes 24584 | tf_op jit(solution)/shard_map/ppermute | solution.py:245

commit v2 on v1

v2 whole, which is shorter than its diff:
```python
import jax
import jax.numpy as jnp
from jax import lax
from jax.experimental import pallas as pl
from jax.experimental.pallas import tpu as pltpu
from jax.sharding import PartitionSpec as P

reg_weight = 0.02
sh_zero = 0.282095
sh_one = 0.488603
sh_two = 1.092548
sh_three = 0.315392
sh_four = 0.546274

AXES = ("gx", "gy", "gz")
LANES = 128
ROWS = 8
PAD = 8
PARAMS = pltpu.CompilerParams(vmem_limit_bytes=40 * 1024 * 1024)


def lane_ids(rows):
    return lax.broadcasted_iota(jnp.int32, (rows, LANES), 1)


def fold(tall, width):
    parts = LANES // width
    rows = tall.shape[0] // parts
    lanes = lane_ids(rows)
    out = tall[:rows]
    for g in range(1, parts):
        moved = pltpu.roll(tall[g * rows : (g + 1) * rows], g * width, 1)
        out = jnp.where((lanes >= g * width) & (lanes < (g + 1) * width), moved, out)
    return out


def unfold(packed, width):
    parts = LANES // width
    pieces = [packed] + [pltpu.roll(packed, LANES - g * width, 1) for g in range(1, parts)]
    return jnp.concatenate(pieces, axis=0)


def edge_flags():
    flags = []
    for axis in AXES:
        index, count = lax.axis_index(axis), lax.axis_size(axis)
        flags.append(
            (
                lax.rem(index, 2) == 0,
                jnp.where(index > 0, 1.0, 0.0).astype(jnp.float32),
                jnp.where(index < count - 1, 1.0, 0.0).astype(jnp.float32),
            )
        )
    return flags


def sides(flag, first, second):
    even, before, after = flag
    return jnp.where(even, second, first) * before, jnp.where(even, first, second) * after


def both_sides(flag, first, second, width):
    before, after = sides(flag, first, second)
    odd = lax.rem(lane_ids(first.shape[0]), 2) == 1
    return unfold(jnp.where(odd, before, after), width)


def pack_kernel(d_hbm, v_hbm, x1, x2, y1, y2, zm, d_ref, v_ref, sems):
    nx, ny, nz = d_ref.shape
    half = nx // 2
    copies = []
    for f, (src, dst) in enumerate(((d_hbm, d_ref), (v_hbm, v_ref))):
        for h in range(2):
            part = pl.ds(h * half, half)
            copy = pltpu.make_async_copy(src.at[part], dst.at[part], sems.at[f, h])
            copy.start()
            copies.append(copy)
    (xe, _, _), (ye, _, _), _ = edge_flags()
    lanes = lane_ids(ny)
    edge = lanes == 0
    pair = lanes // 2
    packed = jnp.zeros((ny, LANES), jnp.float32)
    for f, ref in enumerate((d_ref, v_ref)):
        for h in range(2):
            copies[2 * f + h].wait()
            for x in range(h * half, (h + 1) * half):
                top, bottom = ref[x, ny - 1 : ny, :], ref[x, 0:1, :]
                y1[f, x : x + 1, :] = jnp.where(ye, top, bottom)
                y2[f, x : x + 1, :] = jnp.where(ye, bottom, top)
                plane = ref[x]
                slot = f * nx + x
                up = pltpu.roll(plane, (2 * slot + 2) % LANES, 1)
                down = pltpu.roll(plane, 2 * slot, 1) if slot else plane
                odd = lanes == 2 * slot + 1
                packed = jnp.where(odd, up, jnp.where(lanes == 2 * slot, down, packed))
        x1[f] = jnp.where(xe, ref[nx - 1], ref[0])
        x2[f] = jnp.where(xe, ref[0], ref[nx - 1])
    zm[...] = fold(packed, 4 * nx)


def main_kernel(
    light, d_ref, a_ref, i_ref, v_ref, x1, x2, y1, y2, z1, z2,
    gp, hp, mx1, mx2, my1, my2, mz, sums,
    dpad, vpad, halo, cent, ay, by, bx, zm, myu, myd, accs,
):
    nx, ny, nz = d_ref.shape
    fx, fy, fz = edge_flags()
    for f, (ref, pad) in enumerate(((d_ref, dpad), (v_ref, vpad))):
        pad[1 : nx + 1, PAD : PAD + ny, :] = ref[...]
        before, after = sides(fx, x1[f], x2[f])
        pad[0, PAD : PAD + ny, :] = before
        pad[nx + 1, PAD : PAD + ny, :] = after
        before, after = sides(fy, y1[f], y2[f])
        for x in range(nx):
            pad[x + 1, PAD - 1 : PAD, :] = before[x : x + 1]
            pad[x + 1, PAD + ny : PAD + ny + 1, :] = after[x : x + 1]
    halo[...] = both_sides(fz, z1[...], z2[...], 4 * nx)
    zero_row = jnp.zeros((1, LANES), jnp.float32)
    for u in range(2):
        ay[u, PAD + ny : PAD + ny + 1, :] = zero_row
        by[u, PAD - 1 : PAD, :] = zero_row
    zero = jnp.zeros((ROWS, LANES), jnp.float32)
    zm[...] = jnp.zeros((ny, LANES), jnp.float32)
    bx[...] = jnp.zeros(bx.shape, jnp.float32)
    gp[0] = jnp.zeros((ny, LANES), jnp.float32)
    hp[0] = jnp.zeros((ny, LANES), jnp.float32)
    for k in range(accs.shape[0]):
        accs[k] = zero

    l = [light[k] for k in range(9)]
    c1, c2, c3 = sh_one * l[1], sh_one * l[2], sh_one * l[3]
    c4, c5, c7 = sh_two * l[4], sh_two * l[5], sh_two * l[7]
    c6, c8 = 6.0 * sh_three * l[6], 2.0 * sh_four * l[8]
    base = sh_zero * l[0] - sh_three * l[6]
    lanes = lane_ids(ROWS)
    first, final, pair = lanes == 0, lanes == LANES - 1, lanes // 2

    def shifted(pad, f, x, at, mid):
        xm = pad[x, at : at + ROWS, :]
        xq = pad[x + 2, at : at + ROWS, :]
        ym = pad[x + 1, at - 1 : at - 1 + ROWS, :]
        yq = pad[x + 1, at + 1 : at + 1 + ROWS, :]
        lane = f * nx + x
        rows = slice(at - PAD, at - PAD + ROWS)
        edges = pltpu.roll(halo[rows, :], LANES - 1 - 2 * lane, 1)
        below = jnp.where(first, edges, pltpu.roll(mid, 1, 1))
        above = jnp.where(final, edges, pltpu.roll(mid, LANES - 1, 1))
        lap = (xm + xq) + (ym + yq) + (below + above) - 6.0 * mid
        return xq - xm, yq - ym, above - below, lap

    def plane(x, _):
        for c in range(ny // ROWS):
            at = PAD + c * ROWS
            rows = slice(c * ROWS, (c + 1) * ROWS)
            mid = dpad[x + 1, at : at + ROWS, :]
            hx, hy, hz, lap = shifted(dpad, 0, x, at, mid)
            inv = lax.rsqrt(hx * hx + hy * hy + hz * hz + 1.0)
            nrx, nry, nrz = hx * inv, hy * inv, hz * inv
            px = c3 + c4 * nry + c7 * nrz + c8 * nrx
            py = c1 + c4 * nrx + c5 * nrz - c8 * nry
            pz = c2 + c5 * nry + c7 * nrx + c6 * nrz
            along = nrx * px + nry * py + nrz * pz
            linear = c1 * nry + c2 * nrz + c3 * nrx
            shade = base + 0.5 * (along + linear)
            albedo = a_ref[x, rows, :]
            res = albedo * shade - i_ref[x, rows, :]
            qx, qy, qz = px - nrx * along, py - nry * along, pz - nrz * along
            scale = albedo * inv
            w = albedo * res
            wx, wy, wz = w * nrx, w * nry, w * nrz
            terms = (
                w, wy, wz, wx, wx * nry, wy * nrz, wz * nrz, wx * nrz,
                wx * nrx - wy * nry, res * res + reg_weight * (lap * lap),
            )
            for k, term in enumerate(terms):
                accs[k] = accs[k] + term
            vmid = vpad[x + 1, at : at + ROWS, :]
            ux, uy, uz, vlap = shifted(vpad, 1, x, at, vmid)
            lin = scale * (qx * ux + qy * uy + qz * uz)
            for u, (weight, lapl) in enumerate(((res * scale, lap), (lin * scale, vlap))):
                reg = reg_weight * lapl
                rx, ry, rz = weight * qx, weight * qy, weight * qz
                ay[u, at : at + ROWS, :] = reg - ry
                by[u, at : at + ROWS, :] = reg + ry
                lane = u * nx + x
                fwd = pltpu.roll(reg + rz, 1, 1)
                bwd = pltpu.roll(reg - rz, LANES - 1, 1)
                edges = pltpu.roll(jnp.where(first, fwd, bwd), 2 * lane + 1, 1)
                zm[rows, :] = jnp.where(pair == lane, edges, zm[rows, :])
                out = (gp, hp)[u]
                out[x, rows, :] = out[x, rows, :] + (reg - rx)
                cent[u, rows, :] = (
                    bx[u, rows, :]
                    - 6.0 * reg
                    + jnp.where(first, 0.0, fwd)
                    + jnp.where(final, 0.0, bwd)
                )
                bx[u, rows, :] = reg + rx
        for u in range(2):
            out = (gp, hp)[u]
            for c in range(ny // ROWS):
                at = PAD + c * ROWS
                rows = slice(c * ROWS, (c + 1) * ROWS)
                out[x + 1, rows, :] = (
                    cent[u, rows, :]
                    + ay[u, at + 1 : at + 1 + ROWS, :]
                    + by[u, at - 1 : at - 1 + ROWS, :]
                )
            myd[u, pl.ds(x, 1), :] = ay[u, PAD : PAD + 1, :]
            myu[u, pl.ds(x, 1), :] = by[u, PAD + ny - 1 : PAD + ny, :]
        return 0

    lax.fori_loop(0, nx, plane, 0)
    for u in range(2):
        low = (gp, hp)[u][0]
        mx1[u] = jnp.where(fx[0], bx[u], low)
        mx2[u] = jnp.where(fx[0], low, bx[u])
        my1[u] = jnp.where(fy[0], myu[u], myd[u])
        my2[u] = jnp.where(fy[0], myd[u], myu[u])
    mz[...] = fold(zm[...], 4 * nx)
    line = lax.broadcasted_iota(jnp.int32, (1, LANES), 1)
    row = jnp.zeros((1, LANES), jnp.float32)
    for k in range(accs.shape[0]):
        row = jnp.where(line == k, jnp.sum(accs[k]), row)
    sums[...] = jnp.broadcast_to(row, sums.shape)


def final_kernel(count, all_sums, v_ref, gp, hp, x1, x2, y1, y2, z1, z2, g_ref, h_ref, t_ref, halo):
    nx, ny, nz = v_ref.shape
    fx, fy, fz = edge_flags()
    row = jnp.sum(all_sums[...], axis=0, keepdims=True)
    line = lax.broadcasted_iota(jnp.int32, (1, LANES), 1)
    damping = jnp.sum(jnp.where(line == 9, row, 0.0)) * (0.5 / count)
    weight = jnp.where(line == 0, sh_zero, 0.0)
    for k, factor in enumerate((sh_one, sh_one, sh_one, sh_two, sh_two, 3.0 * sh_three, sh_two, sh_four)):
        weight = jnp.where(line == k + 1, factor, weight)
    shift = jnp.sum(jnp.where(line == 0, row, 0.0)) * sh_three
    t_ref[...] = (row * weight - jnp.where(line == 6, shift, 0.0))[0, :9]
    halo[...] = both_sides(fz, z1[...], z2[...], 4 * nx)
    lanes = lane_ids(ny)
    outer = (lanes == 0) | (lanes == LANES - 1)
    for u, (ref, out) in enumerate(((gp, g_ref), (hp, h_ref))):
        left, right = sides(fx, x1[u], x2[u])
        before, after = sides(fy, y1[u], y2[u])
        for x in range(nx):
            lane = u * nx + x
            value = ref[x + 1]
            value = value + jnp.where(outer, pltpu.roll(halo[...], LANES - 1 - 2 * lane, 1), 0.0)
            if u == 1:
                value = value + damping * v_ref[x]
            if x == 0:
                value = value + left
            if x == nx - 1:
                value = value + right
            out[x] = value
            out[x, 0:1, :] = out[x, 0:1, :] + before[x : x + 1]
            out[x, ny - 1 : ny, :] = out[x, ny - 1 : ny, :] + after[x : x + 1]


def exchange(firsts, seconds):
    got = []
    for axis, one, two in zip(AXES, firsts, seconds):
        count = lax.axis_size(axis)
        inner = [(i, i ^ 1) for i in range(count)]
        outer = [(i, ((((i + 1) % count) ^ 1) - 1) % count) for i in range(count)]
        got.append(lax.ppermute(one, axis, inner))
        got.append(lax.ppermute(two, axis, outer))
    return got


def body(sdf, albedo, intensity, direction, lighting):
    nx, ny, nz = sdf.shape
    devices = 1
    for axis in AXES:
        devices *= lax.axis_size(axis)
    count = float(nx * ny * nz) * devices
    f32 = lambda *shape: jax.ShapeDtypeStruct(shape, jnp.float32)
    rows = ny * 4 * nx // LANES
    faces = [f32(2, ny, nz)] * 2 + [f32(2, nx, nz)] * 2 + [f32(rows, LANES)]
    vmem = pl.BlockSpec(memory_space=pltpu.VMEM)
    smem = pl.BlockSpec(memory_space=pltpu.SMEM)
    scratch = lambda *shape: pltpu.VMEM(shape, jnp.float32)
    tall = ny + 2 * PAD

    x1, x2, y1, y2, zm = pl.pallas_call(
        pack_kernel,
        out_shape=faces,
        in_specs=[pl.BlockSpec(memory_space=pl.ANY)] * 2,
        out_specs=[vmem] * 5,
        scratch_shapes=[scratch(nx, ny, nz), scratch(nx, ny, nz), pltpu.SemaphoreType.DMA((2, 2))],
        compiler_params=PARAMS,
    )(sdf, direction)
    halos = exchange((x1, y1, zm), (x2, y2, zm))
    gp, hp, x1, x2, y1, y2, zm, sums = pl.pallas_call(
        main_kernel,
        out_shape=[f32(nx + 1, ny, nz)] * 2 + faces + [f32(devices, LANES)],
        in_specs=[smem] + [vmem] * 10,
        out_specs=[vmem] * 8,
        scratch_shapes=[
            scratch(nx + 2, tall, nz), scratch(nx + 2, tall, nz), scratch(ny, LANES),
            scratch(2, ny, nz), scratch(2, tall, nz), scratch(2, tall, nz), scratch(2, ny, nz),
            scratch(ny, LANES), scratch(2, nx, nz), scratch(2, nx, nz), scratch(10, ROWS, LANES),
        ],
        compiler_params=PARAMS,
    )(lighting, sdf, albedo, intensity, direction, *halos)
    halos = exchange((x1, y1, zm), (x2, y2, zm))
    all_sums = lax.all_to_all(sums, AXES, 0, 0, tiled=True)
    gradient, hess_vec, totals = pl.pallas_call(
        lambda *refs: final_kernel(count, *refs),
        out_shape=[f32(nx, ny, nz)] * 2 + [f32(9)],
        in_specs=[vmem] * 10,
        out_specs=[vmem] * 3,
        scratch_shapes=[scratch(ny, LANES)],
        compiler_params=PARAMS,
    )(all_sums, direction, gp, hp, *halos)
    return gradient, hess_vec, totals


def solution(mesh):
    grid = P("gx", "gy", "gz")
    return jax.shard_map(
        body,
        mesh=mesh,
        in_specs=(grid, grid, grid, grid, P()),
        out_specs=(grid, grid, P()),
        check_vma=False,
    )
```

time: 54.3 us -> 51 us (0.939); the launches traced: 53.5 us -> 50.8 us
  starting transfers between devices: 37.8 us -> 32.7 us
  waiting for transfers between devices: 2.87 us -> 5.77 us
    all_to_all x1, starting transfers between devices: 13.9 us -> 8.22 us  [body(): all_sums = lax.all_to_all(sums, AXES, 0, 0, tiled=True)]
    ppermute x12, waiting for transfers between devices: 2.05 us -> 5.77 us  [the longest x6 4.01 us: exchange(): got.append(lax.ppermute(two, axis, outer))]
    all_to_all x1, waiting for transfers between devices: 0.82 us -> 0.01 us  [body(): all_sums = lax.all_to_all(sums, AXES, 0, 0, tiled=True)]
    ppermute x12, starting transfers between devices: 23.9 us -> 24.5 us  [the longest x6 15.9 us: exchange(): got.append(lax.ppermute(two, axis, outer))]
where the time goes in v2:
time: 51 us; the launch traced here: 50.8 us
  starting transfers between devices  32.7 us (64%)
  Pallas kernels  9.51 us (19%)
  waiting for transfers between devices  5.77 us (11%)
  local copies, waits for them, and re-layouts  2.1 us (4%)
  between operations  0.71 us (1%)
    ppermute x6, starting transfers between devices, exchange(): got.append(lax.ppermute(two, axis, outer))  15.9 us
    ppermute x6, starting transfers between devices, exchange(): got.append(lax.ppermute(one, axis, inner))  8.54 us
    all_to_all x1, starting transfers between devices, body(): all_sums = lax.all_to_all(sums, AXES, 0, 0, tiled=True)  8.22 us
    pallas_call x1, Pallas kernels, body(): pl.pallas_call(main_kernel, out_shape=[f32(nx + 1, ny, nz)] * 2 + faces +...  7.21 us
    ppermute x6, waiting for transfers between devices, exchange(): got.append(lax.ppermute(two, axis, outer))  4.01 us
    unnamed x12, local copies, waits for them, and re-layouts  2.1 us
    ppermute x6, waiting for transfers between devices, exchange(): got.append(lax.ppermute(one, axis, inner))  1.76 us
    pallas_call x1, Pallas kernels, body(): pl.pallas_call(lambda *refs: final_kernel(count, *refs), out_shape=[f32(n...  1.32 us
  transfers between devices with their start and end apart: 13, of which 4 were waited for; matrix products, arithmetic and copies ran while one was open for 0% of the time, Pallas kernels for 0%

profile of v2, /device:TPU:1, one launch (start us, length us, event | category | flops | bytes accessed | tf_op | source)
XLA Modules:
  0.0 50.8 jit_solution(12917263290448251480)
XLA Ops:
  0.6 0.0 copy-start
  0.6 1.0 %copy-done = f32[16,64,128]{2,1,0:T(8,128)S(1)} copy-done((f32[16,64,128]{2,1,0:T(8,128)S(1)}, f32[16,64,128]{2,1,0:T(8,128)}, u32[]{:S(2)}) %copy-start) | copy-done | bytes 524312
  1.7 0.0 copy-start.2
  1.7 1.0 %copy-done.2 = f32[16,64,128]{2,1,0:T(8,128)S(1)} copy-done((f32[16,64,128]{2,1,0:T(8,128)S(1)}, f32[16,64,128]{2,1,0:T(8,128)}, u32[]{:S(2)}) %copy-start.2) | copy-done | bytes 524312
  2.7 0.0 copy-start.3
  2.7 0.0 copy-start.4
  2.7 1.0 %shard_map.76 = (f32[2,64,128]{2,1,0:T(8,128)S(1)}, f32[2,64,128]{2,1,0:T(8,128)S(1)}, f32[2,16,128]{2,1,0:T(8,128)S(1)}, f32[2,16,128]{2,1,0:T(8,128)S(1)}, f32[32,128]{1,0:T(8,128)S(1)}) custom-call(f32[16,64,128]{2,1,0:T(8,128)S(1)} %copy-done.2, f32[16,64,128]{2,1,0:T(8,128)S(1)} %copy-done), custom_call_target="tpu_custom_call" | custom-call | tf_op jit(solution)/shard_map/pallas_call | solution.py:285
  3.7 3.3 %collective-permute-start = (f32[2,64,128]{2,1,0:T(8,128)S(1)}, f32[2,64,128]{2,1,0:T(8,128)S(1)}, u32[]{:S(2)}, u32[]{:S(2)}) collective-permute-start(f32[2,64,128]{2,1,0:T(8,128)S(1)} %get-tuple-element.16), channel_id=1, source_target_pairs={{0,64},{64,0},{128,192},{192,128},{1,65},{65,1},{129,193},{193,129... | collective-permute-start | bytes 196616 | tf_op jit(solution)/shard_map/ppermute | solution.py:266
  7.0 1.0 %collective-permute-start.1 = (f32[2,64,128]{2,1,0:T(8,128)S(1)}, f32[2,64,128]{2,1,0:T(8,128)S(1)}, u32[]{:S(2)}, u32[]{:S(2)}) collective-permute-start(f32[2,64,128]{2,1,0:T(8,128)S(1)} %get-tuple-element.17), channel_id=1, source_target_pairs={{0,192},{64,128},{128,64},{192,0},{1,193},{65,129},{129,65},{193,1... | collective-permute-start | bytes 196616 | tf_op jit(solution)/shard_map/ppermute | solution.py:267
  8.0 1.6 %collective-permute-start.2 = (f32[2,16,128]{2,1,0:T(8,128)S(1)}, f32[2,16,128]{2,1,0:T(8,128)S(1)}, u32[]{:S(2)}, u32[]{:S(2)}) collective-permute-start(f32[2,16,128]{2,1,0:T(8,128)S(1)} %get-tuple-element.18), channel_id=1, source_target_pairs={{0,8},{8,0},{16,24},{24,16},{32,40},{40,32},{48,56},{56,48},{1,9},... | collective-permute-start | bytes 49160 | tf_op jit(solution)/shard_map/ppermute | solution.py:266
  9.7 0.0 copy-start.5
  9.7 4.7 %collective-permute-start.3 = (f32[2,16,128]{2,1,0:T(8,128)S(1)}, f32[2,16,128]{2,1,0:T(8,128)S(1)}, u32[]{:S(2)}, u32[]{:S(2)}) collective-permute-start(f32[2,16,128]{2,1,0:T(8,128)S(1)} %get-tuple-element.19), channel_id=1, source_target_pairs={{0,56},{8,16},{16,8},{24,32},{32,24},{40,48},{48,40},{56,0},{1,57}... | collective-permute-start | bytes 49160 | tf_op jit(solution)/shard_map/ppermute | solution.py:267
  14.3 2.8 %collective-permute-start.5 = (f32[32,128]{1,0:T(8,128)S(1)}, f32[32,128]{1,0:T(8,128)S(1)}, u32[]{:S(2)}, u32[]{:S(2)}) collective-permute-start(f32[32,128]{1,0:T(8,128)S(1)} %get-tuple-element.20), channel_id=1, source_target_pairs={{0,7},{1,2},{2,1},{3,4},{4,3},{5,6},{6,5},{7,0},{8,15},{9,10},{10,... | collective-permute-start | bytes 49160 | tf_op jit(solution)/shard_map/ppermute | solution.py:267
  17.1 0.0 collective-permute-done.2.y1
  17.1 0.0 collective-permute-start.4
  17.1 0.0 collective-permute-done.3.y2
  17.1 1.9 %collective-permute-done.5.z2 = f32[32,128]{1,0:T(8,128)S(1)} collective-permute-done((f32[32,128]{1,0:T(8,128)S(1)}, f32[32,128]{1,0:T(8,128)S(1)}, u32[]{:S(2)}, u32[]{:S(2)}) %collective-permute-start.5) | collective-permute-done | bytes 16416 | tf_op jit(solution)/shard_map/ppermute | solution.py:267
  19.0 1.0 %collective-permute-done.4.z1 = f32[32,128]{1,0:T(8,128)S(1)} collective-permute-done((f32[32,128]{1,0:T(8,128)S(1)}, f32[32,128]{1,0:T(8,128)S(1)}, u32[]{:S(2)}, u32[]{:S(2)}) %collective-permute-start.4) | collective-permute-done | bytes 16416 | tf_op jit(solution)/shard_map/ppermute | solution.py:266
  20.0 0.0 collective-permute-done.x1
  20.0 0.0 collective-permute-done.1.x2
  20.0 0.0 copy-done.3
  20.0 0.0 copy-done.4
  20.0 0.0 copy-done.5
  20.0 0.0 copy-start.1
  20.0 7.2 %shard_map.77 = (f32[17,64,128]{2,1,0:T(8,128)S(1)}, f32[17,64,128]{2,1,0:T(8,128)S(1)}, f32[2,64,128]{2,1,0:T(8,128)S(1)}, f32[2,64,128]{2,1,0:T(8,128)S(1)}, f...) custom-call(f32[9]{0:T(128)S(1)} %copy-done.5, ...), custom_call_target="tpu_custom_call" | custom-call | tf_op jit(solution)/shard_map/pallas_call | solution.py:294
  27.2 8.2 %all-to-all-start = ((f32[256,1,128]{2,1,0:T(1,128)}), f32[256,1,128]{2,1,0:T(1,128)S(1)}, u32[]{:S(2)}, u32[]{:S(2)}) async-start(f32[256,1,128]{2,1,0:T(1,128)} %bitcast.1), calls=%async_computation | async-start | bytes 262144 | tf_op jit(solution)/shard_map/all_to_all | solution.py:307
  35.5 2.2 %collective-permute-start.6 = (f32[2,64,128]{2,1,0:T(8,128)S(1)}, f32[2,64,128]{2,1,0:T(8,128)S(1)}, u32[]{:S(2)}, u32[]{:S(2)}) collective-permute-start(f32[2,64,128]{2,1,0:T(8,128)S(1)} %get-tuple-element.24), channel_id=1, source_target_pairs={{0,64},{64,0},{128,192},{192,128},{1,65},{65,1},{129,193},{193,129... | collective-permute-start | bytes 196616 | tf_op jit(solution)/shard_map/ppermute | solution.py:266
  37.7 1.2 %collective-permute-start.7 = (f32[2,64,128]{2,1,0:T(8,128)S(1)}, f32[2,64,128]{2,1,0:T(8,128)S(1)}, u32[]{:S(2)}, u32[]{:S(2)}) collective-permute-start(f32[2,64,128]{2,1,0:T(8,128)S(1)} %get-tuple-element.25), channel_id=1, source_target_pairs={{0,192},{64,128},{128,64},{192,0},{1,193},{65,129},{129,65},{193,1... | collective-permute-start | bytes 196616 | tf_op jit(solution)/shard_map/ppermute | solution.py:267
  38.9 1.3 %collective-permute-start.8 = (f32[2,16,128]{2,1,0:T(8,128)S(1)}, f32[2,16,128]{2,1,0:T(8,128)S(1)}, u32[]{:S(2)}, u32[]{:S(2)}) collective-permute-start(f32[2,16,128]{2,1,0:T(8,128)S(1)} %get-tuple-element.26), channel_id=1, source_target_pairs={{0,8},{8,0},{16,24},{24,16},{32,40},{40,32},{48,56},{56,48},{1,9},... | collective-permute-start | bytes 49160 | tf_op jit(solution)/shard_map/ppermute | solution.py:266
  40.2 3.7 %collective-permute-start.9 = (f32[2,16,128]{2,1,0:T(8,128)S(1)}, f32[2,16,128]{2,1,0:T(8,128)S(1)}, u32[]{:S(2)}, u32[]{:S(2)}) collective-permute-start(f32[2,16,128]{2,1,0:T(8,128)S(1)} %get-tuple-element.27), channel_id=1, source_target_pairs={{0,56},{8,16},{16,8},{24,32},{32,24},{40,48},{48,40},{56,0},{1,57}... | collective-permute-start | bytes 49160 | tf_op jit(solution)/shard_map/ppermute | solution.py:267
  43.9 2.6 %collective-permute-start.11 = (f32[32,128]{1,0:T(8,128)S(1)}, f32[32,128]{1,0:T(8,128)S(1)}, u32[]{:S(2)}, u32[]{:S(2)}) collective-permute-start(f32[32,128]{1,0:T(8,128)S(1)} %get-tuple-element.28), channel_id=1, source_target_pairs={{0,7},{1,2},{2,1},{3,4},{4,3},{5,6},{6,5},{7,0},{8,15},{9,10},{10,... | collective-permute-start | bytes 49160 | tf_op jit(solution)/shard_map/ppermute | solution.py:267
  46.5 0.0 collective-permute-done.8.refs_6_
  46.5 0.0 collective-permute-start.10
  46.6 0.0 collective-permute-done.9.refs_7_
  46.6 2.1 %collective-permute-done.11.refs_9_ = f32[32,128]{1,0:T(8,128)S(1)} collective-permute-done((f32[32,128]{1,0:T(8,128)S(1)}, f32[32,128]{1,0:T(8,128)S(1)}, u32[]{:S(2)}, u32[]{:S(2)}) %collective-permute-start.11) | collective-permute-done | bytes 16416 | tf_op jit(solution)/shard_map/ppermute | solution.py:267
  48.6 0.8 %collective-permute-done.10.refs_8_ = f32[32,128]{1,0:T(8,128)S(1)} collective-permute-done((f32[32,128]{1,0:T(8,128)S(1)}, f32[32,128]{1,0:T(8,128)S(1)}, u32[]{:S(2)}, u32[]{:S(2)}) %collective-permute-start.10) | collective-permute-done | bytes 16416 | tf_op jit(solution)/shard_map/ppermute | solution.py:266
  49.4 0.0 collective-permute-done.6.refs_4_
  49.4 0.0 collective-permute-done.7.refs_5_
  49.4 0.0 all-to-all-done
  49.4 0.0 copy-done.1
  49.5 1.3 %shard_map.78 = (f32[16,64,128]{2,1,0:T(8,128)}, f32[16,64,128]{2,1,0:T(8,128)}, f32[9]{0:T(128)}) custom-call(f32[256,128]{1,0:T(8,128)S(1)} %bitcast.4, f32[16,64,128]{2,1,0:T(8,128)S(1)} %copy-done.1, f32[17,64,128]{2,1,0:T(8,128)S(1)} %get-tuple-element.22.refs_2_, f32[17,64,128]{2,1,0:T(8,128)S(1)} %get-tuple-element.23.refs_3_, ...), custom_call_target="tpu_custom_call" | custom-call | tf_op jit(solution)/shard_map/pallas_call | solution.py:308
Async XLA Ops:
  0.6 1.0 %copy-start = (f32[16,64,128]{2,1,0:T(8,128)S(1)}, f32[16,64,128]{2,1,0:T(8,128)}, u32[]{:S(2)}) copy-start(f32[16,64,128]{2,1,0:T(8,128)} %refs_1_.1) | copy-start | bytes 1572868
  1.7 1.0 %copy-start.2 = (f32[16,64,128]{2,1,0:T(8,128)S(1)}, f32[16,64,128]{2,1,0:T(8,128)}, u32[]{:S(2)}) copy-start(f32[16,64,128]{2,1,0:T(8,128)} %d_ref.1) | copy-start | bytes 1572868
  2.7 17.3 %copy-start.3 = (f32[16,64,128]{2,1,0:T(8,128)S(1)}, f32[16,64,128]{2,1,0:T(8,128)}, u32[]{:S(2)}) copy-start(f32[16,64,128]{2,1,0:T(8,128)} %a_ref.1) | copy-start | bytes 1572868
  2.7 17.3 %copy-start.4 = (f32[16,64,128]{2,1,0:T(8,128)S(1)}, f32[16,64,128]{2,1,0:T(8,128)}, u32[]{:S(2)}) copy-start(f32[16,64,128]{2,1,0:T(8,128)} %i_ref.1) | copy-start | bytes 1572868
  3.7 16.3 %collective-permute-start = (f32[2,64,128]{2,1,0:T(8,128)S(1)}, f32[2,64,128]{2,1,0:T(8,128)S(1)}, u32[]{:S(2)}, u32[]{:S(2)}) collective-permute-start(f32[2,64,128]{2,1,0:T(8,128)S(1)} %get-tuple-element.16), channel_id=1, source_target_pairs={{0,64},{64,0},{128,192},{192,128},{1,65},{65,1},{129,193},{193,129... | collective-permute-start | bytes 196616 | tf_op jit(solution)/shard_map/ppermute | solution.py:266
  7.0 13.0 %collective-permute-start.1 = (f32[2,64,128]{2,1,0:T(8,128)S(1)}, f32[2,64,128]{2,1,0:T(8,128)S(1)}, u32[]{:S(2)}, u32[]{:S(2)}) collective-permute-start(f32[2,64,128]{2,1,0:T(8,128)S(1)} %get-tuple-element.17), channel_id=1, source_target_pairs={{0,192},{64,128},{128,64},{192,0},{1,193},{65,129},{129,65},{193,1... | collective-permute-start | bytes 196616 | tf_op jit(solution)/shard_map/ppermute | solution.py:267
  8.0 9.1 %collective-permute-start.2 = (f32[2,16,128]{2,1,0:T(8,128)S(1)}, f32[2,16,128]{2,1,0:T(8,128)S(1)}, u32[]{:S(2)}, u32[]{:S(2)}) collective-permute-start(f32[2,16,128]{2,1,0:T(8,128)S(1)} %get-tuple-element.18), channel_id=1, source_target_pairs={{0,8},{8,0},{16,24},{24,16},{32,40},{40,32},{48,56},{56,48},{1,9},... | collective-permute-start | bytes 49160 | tf_op jit(solution)/shard_map/ppermute | solution.py:266
  9.7 10.3 %copy-start.5 = (f32[9]{0:T(128)S(1)}, f32[9]{0:T(128)}, u32[]{:S(2)}) copy-start(f32[9]{0:T(128)} %light.1) | copy-start | bytes 112
  9.7 7.4 %collective-permute-start.3 = (f32[2,16,128]{2,1,0:T(8,128)S(1)}, f32[2,16,128]{2,1,0:T(8,128)S(1)}, u32[]{:S(2)}, u32[]{:S(2)}) collective-permute-start(f32[2,16,128]{2,1,0:T(8,128)S(1)} %get-tuple-element.19), channel_id=1, source_target_pairs={{0,56},{8,16},{16,8},{24,32},{32,24},{40,48},{48,40},{56,0},{1,57}... | collective-permute-start | bytes 49160 | tf_op jit(solution)/shard_map/ppermute | solution.py:267
  14.3 4.7 %collective-permute-start.5 = (f32[32,128]{1,0:T(8,128)S(1)}, f32[32,128]{1,0:T(8,128)S(1)}, u32[]{:S(2)}, u32[]{:S(2)}) collective-permute-start(f32[32,128]{1,0:T(8,128)S(1)} %get-tuple-element.20), channel_id=1, source_target_pairs={{0,7},{1,2},{2,1},{3,4},{4,3},{5,6},{6,5},{7,0},{8,15},{9,10},{10,... | collective-permute-start | bytes 49160 | tf_op jit(solution)/shard_map/ppermute | solution.py:267
  17.1 2.9 %collective-permute-start.4 = (f32[32,128]{1,0:T(8,128)S(1)}, f32[32,128]{1,0:T(8,128)S(1)}, u32[]{:S(2)}, u32[]{:S(2)}) collective-permute-start(f32[32,128]{1,0:T(8,128)S(1)} %get-tuple-element.20), channel_id=1, source_target_pairs={{0,1},{1,0},{2,3},{3,2},{4,5},{5,4},{6,7},{7,6},{8,9},{9,8},{10,11... | collective-permute-start | bytes 49160 | tf_op jit(solution)/shard_map/ppermute | solution.py:266
  20.0 29.4 %copy-start.1 = (f32[16,64,128]{2,1,0:T(8,128)S(1)}, f32[16,64,128]{2,1,0:T(8,128)}, u32[]{:S(2)}) copy-start(f32[16,64,128]{2,1,0:T(8,128)} %refs_1_.1) | copy-start | bytes 1572868
  27.2 22.2 %all-to-all-start = ((f32[256,1,128]{2,1,0:T(1,128)}), f32[256,1,128]{2,1,0:T(1,128)S(1)}, u32[]{:S(2)}, u32[]{:S(2)}) async-start(f32[256,1,128]{2,1,0:T(1,128)} %bitcast.1), calls=%async_computation | async-start | bytes 262144 | tf_op jit(solution)/shard_map/all_to_all | solution.py:307
  35.5 14.0 %collective-permute-start.6 = (f32[2,64,128]{2,1,0:T(8,128)S(1)}, f32[2,64,128]{2,1,0:T(8,128)S(1)}, u32[]{:S(2)}, u32[]{:S(2)}) collective-permute-start(f32[2,64,128]{2,1,0:T(8,128)S(1)} %get-tuple-element.24), channel_id=1, source_target_pairs={{0,64},{64,0},{128,192},{192,128},{1,65},{65,1},{129,193},{193,129... | collective-permute-start | bytes 196616 | tf_op jit(solution)/shard_map/ppermute | solution.py:266
  37.7 11.7 %collective-permute-start.7 = (f32[2,64,128]{2,1,0:T(8,128)S(1)}, f32[2,64,128]{2,1,0:T(8,128)S(1)}, u32[]{:S(2)}, u32[]{:S(2)}) collective-permute-start(f32[2,64,128]{2,1,0:T(8,128)S(1)} %get-tuple-element.25), channel_id=1, source_target_pairs={{0,192},{64,128},{128,64},{192,0},{1,193},{65,129},{129,65},{193,1... | collective-permute-start | bytes 196616 | tf_op jit(solution)/shard_map/ppermute | solution.py:267
  38.9 7.7 %collective-permute-start.8 = (f32[2,16,128]{2,1,0:T(8,128)S(1)}, f32[2,16,128]{2,1,0:T(8,128)S(1)}, u32[]{:S(2)}, u32[]{:S(2)}) collective-permute-start(f32[2,16,128]{2,1,0:T(8,128)S(1)} %get-tuple-element.26), channel_id=1, source_target_pairs={{0,8},{8,0},{16,24},{24,16},{32,40},{40,32},{48,56},{56,48},{1,9},... | collective-permute-start | bytes 49160 | tf_op jit(solution)/shard_map/ppermute | solution.py:266
  40.2 6.4 %collective-permute-start.9 = (f32[2,16,128]{2,1,0:T(8,128)S(1)}, f32[2,16,128]{2,1,0:T(8,128)S(1)}, u32[]{:S(2)}, u32[]{:S(2)}) collective-permute-start(f32[2,16,128]{2,1,0:T(8,128)S(1)} %get-tuple-element.27), channel_id=1, source_target_pairs={{0,56},{8,16},{16,8},{24,32},{32,24},{40,48},{48,40},{56,0},{1,57}... | collective-permute-start | bytes 49160 | tf_op jit(solution)/shard_map/ppermute | solution.py:267
  43.9 4.7 %collective-permute-start.11 = (f32[32,128]{1,0:T(8,128)S(1)}, f32[32,128]{1,0:T(8,128)S(1)}, u32[]{:S(2)}, u32[]{:S(2)}) collective-permute-start(f32[32,128]{1,0:T(8,128)S(1)} %get-tuple-element.28), channel_id=1, source_target_pairs={{0,7},{1,2},{2,1},{3,4},{4,3},{5,6},{6,5},{7,0},{8,15},{9,10},{10,... | collective-permute-start | bytes 49160 | tf_op jit(solution)/shard_map/ppermute | solution.py:267
  46.5 2.9 %collective-permute-start.10 = (f32[32,128]{1,0:T(8,128)S(1)}, f32[32,128]{1,0:T(8,128)S(1)}, u32[]{:S(2)}, u32[]{:S(2)}) collective-permute-start(f32[32,128]{1,0:T(8,128)S(1)} %get-tuple-element.28), channel_id=1, source_target_pairs={{0,1},{1,0},{2,3},{3,2},{4,5},{5,4},{6,7},{7,6},{8,9},{9,8},{10,11... | collective-permute-start | bytes 49160 | tf_op jit(solution)/shard_map/ppermute | solution.py:266

commit v3 on v2

--- a/solution.py
+++ b/solution.py
@@ -210,7 +210,7 @@
             myu[u, pl.ds(x, 1), :] = by[u, PAD + ny - 1 : PAD + ny, :]
         return 0
 
-    lax.fori_loop(0, nx, plane, 0)
+    lax.fori_loop(0, nx, plane, 0, unroll=2)
     for u in range(2):
         low = (gp, hp)[u][0]
         mx1[u] = jnp.where(fx[0], bx[u], low)
@@ -286,7 +286,7 @@
         pack_kernel,
         out_shape=faces,
         in_specs=[pl.BlockSpec(memory_space=pl.ANY)] * 2,
-        out_specs=[vmem] * 5,
+        out_specs=[vmem] * len(faces),
         scratch_shapes=[scratch(nx, ny, nz), scratch(nx, ny, nz), pltpu.SemaphoreType.DMA((2, 2))],
         compiler_params=PARAMS,
     )(sdf, direction)
@@ -295,7 +295,7 @@
         main_kernel,
         out_shape=[f32(nx + 1, ny, nz)] * 2 + faces + [f32(devices, LANES)],
         in_specs=[smem] + [vmem] * 10,
-        out_specs=[vmem] * 8,
+        out_specs=[vmem] * (len(faces) + 3),
         scratch_shapes=[
             scratch(nx + 2, tall, nz), scratch(nx + 2, tall, nz), scratch(ny, LANES),
             scratch(2, ny, nz), scratch(2, tall, nz), scratch(2, tall, nz), scratch(2, ny, nz),

time: 51 us -> 49.3 us (0.967)
  Pallas kernels: 9.51 us -> 7.79 us
    pallas_call x1, Pallas kernels: 7.21 us -> 5.49 us  [body(): pl.pallas_call(main_kernel, out_shape=[f32(nx + 1, ny, nz)] * 2 + faces +...]
where the time goes in v3:
time: 49.3 us; the launch traced here: 49.1 us
  starting transfers between devices  32.7 us (66%)
  Pallas kernels  7.79 us (16%)
  waiting for transfers between devices  5.77 us (12%)
  local copies, waits for them, and re-layouts  2.1 us (4%)
  between operations  0.71 us (1%)
    ppermute x6, starting transfers between devices, exchange(): got.append(lax.ppermute(two, axis, outer))  15.9 us
    ppermute x6, starting transfers between devices, exchange(): got.append(lax.ppermute(one, axis, inner))  8.54 us
    all_to_all x1, starting transfers between devices, body(): all_sums = lax.all_to_all(sums, AXES, 0, 0, tiled=True)  8.22 us
    pallas_call x1, Pallas kernels, body(): pl.pallas_call(main_kernel, out_shape=[f32(nx + 1, ny, nz)] * 2 + faces +...  5.49 us
    ppermute x6, waiting for transfers between devices, exchange(): got.append(lax.ppermute(two, axis, outer))  4.01 us
    unnamed x12, local copies, waits for them, and re-layouts  2.1 us
    ppermute x6, waiting for transfers between devices, exchange(): got.append(lax.ppermute(one, axis, inner))  1.76 us
    pallas_call x1, Pallas kernels, body(): pl.pallas_call(lambda *refs: final_kernel(count, *refs), out_shape=[f32(n...  1.32 us
  transfers between devices with their start and end apart: 13, of which 4 were waited for; matrix products, arithmetic and copies ran while one was open for 0% of the time, Pallas kernels for 0%

profile of v3, /device:TPU:1, one launch (start us, length us, event | category | flops | bytes accessed | tf_op | source)
XLA Modules:
  0.0 49.1 jit_solution(6885891998702318030)
XLA Ops:
  0.6 0.0 copy-start
  0.6 1.0 %copy-done = f32[16,64,128]{2,1,0:T(8,128)S(1)} copy-done((f32[16,64,128]{2,1,0:T(8,128)S(1)}, f32[16,64,128]{2,1,0:T(8,128)}, u32[]{:S(2)}) %copy-start) | copy-done | bytes 524312
  1.7 0.0 copy-start.2
  1.7 1.0 %copy-done.2 = f32[16,64,128]{2,1,0:T(8,128)S(1)} copy-done((f32[16,64,128]{2,1,0:T(8,128)S(1)}, f32[16,64,128]{2,1,0:T(8,128)}, u32[]{:S(2)}) %copy-start.2) | copy-done | bytes 524312
  2.7 0.0 copy-start.3
  2.7 0.0 copy-start.4
  2.7 1.0 %shard_map.76 = (f32[2,64,128]{2,1,0:T(8,128)S(1)}, f32[2,64,128]{2,1,0:T(8,128)S(1)}, f32[2,16,128]{2,1,0:T(8,128)S(1)}, f32[2,16,128]{2,1,0:T(8,128)S(1)}, f32[32,128]{1,0:T(8,128)S(1)}) custom-call(f32[16,64,128]{2,1,0:T(8,128)S(1)} %copy-done.2, f32[16,64,128]{2,1,0:T(8,128)S(1)} %copy-done), custom_call_target="tpu_custom_call" | custom-call | tf_op jit(solution)/shard_map/pallas_call | solution.py:285
  3.7 3.3 %collective-permute-start = (f32[2,64,128]{2,1,0:T(8,128)S(1)}, f32[2,64,128]{2,1,0:T(8,128)S(1)}, u32[]{:S(2)}, u32[]{:S(2)}) collective-permute-start(f32[2,64,128]{2,1,0:T(8,128)S(1)} %get-tuple-element.16), channel_id=1, source_target_pairs={{0,64},{64,0},{128,192},{192,128},{1,65},{65,1},{129,193},{193,129... | collective-permute-start | bytes 196616 | tf_op jit(solution)/shard_map/ppermute | solution.py:266
  7.0 1.0 %collective-permute-start.1 = (f32[2,64,128]{2,1,0:T(8,128)S(1)}, f32[2,64,128]{2,1,0:T(8,128)S(1)}, u32[]{:S(2)}, u32[]{:S(2)}) collective-permute-start(f32[2,64,128]{2,1,0:T(8,128)S(1)} %get-tuple-element.17), channel_id=1, source_target_pairs={{0,192},{64,128},{128,64},{192,0},{1,193},{65,129},{129,65},{193,1... | collective-permute-start | bytes 196616 | tf_op jit(solution)/shard_map/ppermute | solution.py:267
  8.0 1.6 %collective-permute-start.2 = (f32[2,16,128]{2,1,0:T(8,128)S(1)}, f32[2,16,128]{2,1,0:T(8,128)S(1)}, u32[]{:S(2)}, u32[]{:S(2)}) collective-permute-start(f32[2,16,128]{2,1,0:T(8,128)S(1)} %get-tuple-element.18), channel_id=1, source_target_pairs={{0,8},{8,0},{16,24},{24,16},{32,40},{40,32},{48,56},{56,48},{1,9},... | collective-permute-start | bytes 49160 | tf_op jit(solution)/shard_map/ppermute | solution.py:266
  9.7 0.0 copy-start.5
  9.7 4.7 %collective-permute-start.3 = (f32[2,16,128]{2,1,0:T(8,128)S(1)}, f32[2,16,128]{2,1,0:T(8,128)S(1)}, u32[]{:S(2)}, u32[]{:S(2)}) collective-permute-start(f32[2,16,128]{2,1,0:T(8,128)S(1)} %get-tuple-element.19), channel_id=1, source_target_pairs={{0,56},{8,16},{16,8},{24,32},{32,24},{40,48},{48,40},{56,0},{1,57}... | collective-permute-start | bytes 49160 | tf_op jit(solution)/shard_map/ppermute | solution.py:267
  14.3 2.8 %collective-permute-start.5 = (f32[32,128]{1,0:T(8,128)S(1)}, f32[32,128]{1,0:T(8,128)S(1)}, u32[]{:S(2)}, u32[]{:S(2)}) collective-permute-start(f32[32,128]{1,0:T(8,128)S(1)} %get-tuple-element.20), channel_id=1, source_target_pairs={{0,7},{1,2},{2,1},{3,4},{4,3},{5,6},{6,5},{7,0},{8,15},{9,10},{10,... | collective-permute-start | bytes 49160 | tf_op jit(solution)/shard_map/ppermute | solution.py:267
  17.1 0.0 collective-permute-done.2.y1
  17.1 0.0 collective-permute-start.4
  17.1 0.0 collective-permute-done.3.y2
  17.1 1.9 %collective-permute-done.5.z2 = f32[32,128]{1,0:T(8,128)S(1)} collective-permute-done((f32[32,128]{1,0:T(8,128)S(1)}, f32[32,128]{1,0:T(8,128)S(1)}, u32[]{:S(2)}, u32[]{:S(2)}) %collective-permute-start.5) | collective-permute-done | bytes 16416 | tf_op jit(solution)/shard_map/ppermute | solution.py:267
  19.0 1.0 %collective-permute-done.4.z1 = f32[32,128]{1,0:T(8,128)S(1)} collective-permute-done((f32[32,128]{1,0:T(8,128)S(1)}, f32[32,128]{1,0:T(8,128)S(1)}, u32[]{:S(2)}, u32[]{:S(2)}) %collective-permute-start.4) | collective-permute-done | bytes 16416 | tf_op jit(solution)/shard_map/ppermute | solution.py:266
  20.0 0.0 collective-permute-done.x1
  20.0 0.0 collective-permute-done.1.x2
  20.0 0.0 copy-done.3
  20.0 0.0 copy-done.4
  20.0 0.0 copy-done.5
  20.0 0.0 copy-start.1
  20.0 5.5 %shard_map.77 = (f32[17,64,128]{2,1,0:T(8,128)S(1)}, f32[17,64,128]{2,1,0:T(8,128)S(1)}, f32[2,64,128]{2,1,0:T(8,128)S(1)}, f32[2,64,128]{2,1,0:T(8,128)S(1)}, f...) custom-call(f32[9]{0:T(128)S(1)} %copy-done.5, ...), custom_call_target="tpu_custom_call" | custom-call | tf_op jit(solution)/shard_map/pallas_call | solution.py:294
  25.5 8.2 %all-to-all-start = ((f32[256,1,128]{2,1,0:T(1,128)}), f32[256,1,128]{2,1,0:T(1,128)S(1)}, u32[]{:S(2)}, u32[]{:S(2)}) async-start(f32[256,1,128]{2,1,0:T(1,128)} %bitcast.1), calls=%async_computation | async-start | bytes 262144 | tf_op jit(solution)/shard_map/all_to_all | solution.py:307
  33.7 2.2 %collective-permute-start.6 = (f32[2,64,128]{2,1,0:T(8,128)S(1)}, f32[2,64,128]{2,1,0:T(8,128)S(1)}, u32[]{:S(2)}, u32[]{:S(2)}) collective-permute-start(f32[2,64,128]{2,1,0:T(8,128)S(1)} %get-tuple-element.24), channel_id=1, source_target_pairs={{0,64},{64,0},{128,192},{192,128},{1,65},{65,1},{129,193},{193,129... | collective-permute-start | bytes 196616 | tf_op jit(solution)/shard_map/ppermute | solution.py:266
  36.0 1.2 %collective-permute-start.7 = (f32[2,64,128]{2,1,0:T(8,128)S(1)}, f32[2,64,128]{2,1,0:T(8,128)S(1)}, u32[]{:S(2)}, u32[]{:S(2)}) collective-permute-start(f32[2,64,128]{2,1,0:T(8,128)S(1)} %get-tuple-element.25), channel_id=1, source_target_pairs={{0,192},{64,128},{128,64},{192,0},{1,193},{65,129},{129,65},{193,1... | collective-permute-start | bytes 196616 | tf_op jit(solution)/shard_map/ppermute | solution.py:267
  37.1 1.3 %collective-permute-start.8 = (f32[2,16,128]{2,1,0:T(8,128)S(1)}, f32[2,16,128]{2,1,0:T(8,128)S(1)}, u32[]{:S(2)}, u32[]{:S(2)}) collective-permute-start(f32[2,16,128]{2,1,0:T(8,128)S(1)} %get-tuple-element.26), channel_id=1, source_target_pairs={{0,8},{8,0},{16,24},{24,16},{32,40},{40,32},{48,56},{56,48},{1,9},... | collective-permute-start | bytes 49160 | tf_op jit(solution)/shard_map/ppermute | solution.py:266
  38.5 3.7 %collective-permute-start.9 = (f32[2,16,128]{2,1,0:T(8,128)S(1)}, f32[2,16,128]{2,1,0:T(8,128)S(1)}, u32[]{:S(2)}, u32[]{:S(2)}) collective-permute-start(f32[2,16,128]{2,1,0:T(8,128)S(1)} %get-tuple-element.27), channel_id=1, source_target_pairs={{0,56},{8,16},{16,8},{24,32},{32,24},{40,48},{48,40},{56,0},{1,57}... | collective-permute-start | bytes 49160 | tf_op jit(solution)/shard_map/ppermute | solution.py:267
  42.2 2.6 %collective-permute-start.11 = (f32[32,128]{1,0:T(8,128)S(1)}, f32[32,128]{1,0:T(8,128)S(1)}, u32[]{:S(2)}, u32[]{:S(2)}) collective-permute-start(f32[32,128]{1,0:T(8,128)S(1)} %get-tuple-element.28), channel_id=1, source_target_pairs={{0,7},{1,2},{2,1},{3,4},{4,3},{5,6},{6,5},{7,0},{8,15},{9,10},{10,... | collective-permute-start | bytes 49160 | tf_op jit(solution)/shard_map/ppermute | solution.py:267
  44.8 0.0 collective-permute-done.8.refs_6_
  44.8 0.0 collective-permute-start.10
  44.8 0.0 collective-permute-done.9.refs_7_
  44.8 2.1 %collective-permute-done.11.refs_9_ = f32[32,128]{1,0:T(8,128)S(1)} collective-permute-done((f32[32,128]{1,0:T(8,128)S(1)}, f32[32,128]{1,0:T(8,128)S(1)}, u32[]{:S(2)}, u32[]{:S(2)}) %collective-permute-start.11) | collective-permute-done | bytes 16416 | tf_op jit(solution)/shard_map/ppermute | solution.py:267
  46.9 0.8 %collective-permute-done.10.refs_8_ = f32[32,128]{1,0:T(8,128)S(1)} collective-permute-done((f32[32,128]{1,0:T(8,128)S(1)}, f32[32,128]{1,0:T(8,128)S(1)}, u32[]{:S(2)}, u32[]{:S(2)}) %collective-permute-start.10) | collective-permute-done | bytes 16416 | tf_op jit(solution)/shard_map/ppermute | solution.py:266
  47.7 0.0 collective-permute-done.6.refs_4_
  47.7 0.0 collective-permute-done.7.refs_5_
  47.7 0.0 all-to-all-done
  47.7 0.0 copy-done.1
  47.7 1.3 %shard_map.78 = (f32[16,64,128]{2,1,0:T(8,128)}, f32[16,64,128]{2,1,0:T(8,128)}, f32[9]{0:T(128)}) custom-call(f32[256,128]{1,0:T(8,128)S(1)} %bitcast.4, f32[16,64,128]{2,1,0:T(8,128)S(1)} %copy-done.1, f32[17,64,128]{2,1,0:T(8,128)S(1)} %get-tuple-element.22.refs_2_, f32[17,64,128]{2,1,0:T(8,128)S(1)} %get-tuple-element.23.refs_3_, ...), custom_call_target="tpu_custom_call" | custom-call | tf_op jit(solution)/shard_map/pallas_call | solution.py:308
Async XLA Ops:
  0.6 1.0 %copy-start = (f32[16,64,128]{2,1,0:T(8,128)S(1)}, f32[16,64,128]{2,1,0:T(8,128)}, u32[]{:S(2)}) copy-start(f32[16,64,128]{2,1,0:T(8,128)} %refs_1_.1) | copy-start | bytes 1572868
  1.7 1.0 %copy-start.2 = (f32[16,64,128]{2,1,0:T(8,128)S(1)}, f32[16,64,128]{2,1,0:T(8,128)}, u32[]{:S(2)}) copy-start(f32[16,64,128]{2,1,0:T(8,128)} %d_ref.1) | copy-start | bytes 1572868
  2.7 17.3 %copy-start.3 = (f32[16,64,128]{2,1,0:T(8,128)S(1)}, f32[16,64,128]{2,1,0:T(8,128)}, u32[]{:S(2)}) copy-start(f32[16,64,128]{2,1,0:T(8,128)} %a_ref.1) | copy-start | bytes 1572868
  2.7 17.3 %copy-start.4 = (f32[16,64,128]{2,1,0:T(8,128)S(1)}, f32[16,64,128]{2,1,0:T(8,128)}, u32[]{:S(2)}) copy-start(f32[16,64,128]{2,1,0:T(8,128)} %i_ref.1) | copy-start | bytes 1572868
  3.7 16.3 %collective-permute-start = (f32[2,64,128]{2,1,0:T(8,128)S(1)}, f32[2,64,128]{2,1,0:T(8,128)S(1)}, u32[]{:S(2)}, u32[]{:S(2)}) collective-permute-start(f32[2,64,128]{2,1,0:T(8,128)S(1)} %get-tuple-element.16), channel_id=1, source_target_pairs={{0,64},{64,0},{128,192},{192,128},{1,65},{65,1},{129,193},{193,129... | collective-permute-start | bytes 196616 | tf_op jit(solution)/shard_map/ppermute | solution.py:266
  7.0 13.0 %collective-permute-start.1 = (f32[2,64,128]{2,1,0:T(8,128)S(1)}, f32[2,64,128]{2,1,0:T(8,128)S(1)}, u32[]{:S(2)}, u32[]{:S(2)}) collective-permute-start(f32[2,64,128]{2,1,0:T(8,128)S(1)} %get-tuple-element.17), channel_id=1, source_target_pairs={{0,192},{64,128},{128,64},{192,0},{1,193},{65,129},{129,65},{193,1... | collective-permute-start | bytes 196616 | tf_op jit(solution)/shard_map/ppermute | solution.py:267
  8.0 9.1 %collective-permute-start.2 = (f32[2,16,128]{2,1,0:T(8,128)S(1)}, f32[2,16,128]{2,1,0:T(8,128)S(1)}, u32[]{:S(2)}, u32[]{:S(2)}) collective-permute-start(f32[2,16,128]{2,1,0:T(8,128)S(1)} %get-tuple-element.18), channel_id=1, source_target_pairs={{0,8},{8,0},{16,24},{24,16},{32,40},{40,32},{48,56},{56,48},{1,9},... | collective-permute-start | bytes 49160 | tf_op jit(solution)/shard_map/ppermute | solution.py:266
  9.7 10.3 %copy-start.5 = (f32[9]{0:T(128)S(1)}, f32[9]{0:T(128)}, u32[]{:S(2)}) copy-start(f32[9]{0:T(128)} %light.1) | copy-start | bytes 112
  9.7 7.4 %collective-permute-start.3 = (f32[2,16,128]{2,1,0:T(8,128)S(1)}, f32[2,16,128]{2,1,0:T(8,128)S(1)}, u32[]{:S(2)}, u32[]{:S(2)}) collective-permute-start(f32[2,16,128]{2,1,0:T(8,128)S(1)} %get-tuple-element.19), channel_id=1, source_target_pairs={{0,56},{8,16},{16,8},{24,32},{32,24},{40,48},{48,40},{56,0},{1,57}... | collective-permute-start | bytes 49160 | tf_op jit(solution)/shard_map/ppermute | solution.py:267
  14.3 4.7 %collective-permute-start.5 = (f32[32,128]{1,0:T(8,128)S(1)}, f32[32,128]{1,0:T(8,128)S(1)}, u32[]{:S(2)}, u32[]{:S(2)}) collective-permute-start(f32[32,128]{1,0:T(8,128)S(1)} %get-tuple-element.20), channel_id=1, source_target_pairs={{0,7},{1,2},{2,1},{3,4},{4,3},{5,6},{6,5},{7,0},{8,15},{9,10},{10,... | collective-permute-start | bytes 49160 | tf_op jit(solution)/shard_map/ppermute | solution.py:267
  17.1 2.9 %collective-permute-start.4 = (f32[32,128]{1,0:T(8,128)S(1)}, f32[32,128]{1,0:T(8,128)S(1)}, u32[]{:S(2)}, u32[]{:S(2)}) collective-permute-start(f32[32,128]{1,0:T(8,128)S(1)} %get-tuple-element.20), channel_id=1, source_target_pairs={{0,1},{1,0},{2,3},{3,2},{4,5},{5,4},{6,7},{7,6},{8,9},{9,8},{10,11... | collective-permute-start | bytes 49160 | tf_op jit(solution)/shard_map/ppermute | solution.py:266
  20.0 27.7 %copy-start.1 = (f32[16,64,128]{2,1,0:T(8,128)S(1)}, f32[16,64,128]{2,1,0:T(8,128)}, u32[]{:S(2)}) copy-start(f32[16,64,128]{2,1,0:T(8,128)} %refs_1_.1) | copy-start | bytes 1572868
  25.5 22.2 %all-to-all-start = ((f32[256,1,128]{2,1,0:T(1,128)}), f32[256,1,128]{2,1,0:T(1,128)S(1)}, u32[]{:S(2)}, u32[]{:S(2)}) async-start(f32[256,1,128]{2,1,0:T(1,128)} %bitcast.1), calls=%async_computation | async-start | bytes 262144 | tf_op jit(solution)/shard_map/all_to_all | solution.py:307
  33.7 14.0 %collective-permute-start.6 = (f32[2,64,128]{2,1,0:T(8,128)S(1)}, f32[2,64,128]{2,1,0:T(8,128)S(1)}, u32[]{:S(2)}, u32[]{:S(2)}) collective-permute-start(f32[2,64,128]{2,1,0:T(8,128)S(1)} %get-tuple-element.24), channel_id=1, source_target_pairs={{0,64},{64,0},{128,192},{192,128},{1,65},{65,1},{129,193},{193,129... | collective-permute-start | bytes 196616 | tf_op jit(solution)/shard_map/ppermute | solution.py:266
  36.0 11.7 %collective-permute-start.7 = (f32[2,64,128]{2,1,0:T(8,128)S(1)}, f32[2,64,128]{2,1,0:T(8,128)S(1)}, u32[]{:S(2)}, u32[]{:S(2)}) collective-permute-start(f32[2,64,128]{2,1,0:T(8,128)S(1)} %get-tuple-element.25), channel_id=1, source_target_pairs={{0,192},{64,128},{128,64},{192,0},{1,193},{65,129},{129,65},{193,1... | collective-permute-start | bytes 196616 | tf_op jit(solution)/shard_map/ppermute | solution.py:267
  37.1 7.7 %collective-permute-start.8 = (f32[2,16,128]{2,1,0:T(8,128)S(1)}, f32[2,16,128]{2,1,0:T(8,128)S(1)}, u32[]{:S(2)}, u32[]{:S(2)}) collective-permute-start(f32[2,16,128]{2,1,0:T(8,128)S(1)} %get-tuple-element.26), channel_id=1, source_target_pairs={{0,8},{8,0},{16,24},{24,16},{32,40},{40,32},{48,56},{56,48},{1,9},... | collective-permute-start | bytes 49160 | tf_op jit(solution)/shard_map/ppermute | solution.py:266
  38.5 6.4 %collective-permute-start.9 = (f32[2,16,128]{2,1,0:T(8,128)S(1)}, f32[2,16,128]{2,1,0:T(8,128)S(1)}, u32[]{:S(2)}, u32[]{:S(2)}) collective-permute-start(f32[2,16,128]{2,1,0:T(8,128)S(1)} %get-tuple-element.27), channel_id=1, source_target_pairs={{0,56},{8,16},{16,8},{24,32},{32,24},{40,48},{48,40},{56,0},{1,57}... | collective-permute-start | bytes 49160 | tf_op jit(solution)/shard_map/ppermute | solution.py:267
  42.2 4.7 %collective-permute-start.11 = (f32[32,128]{1,0:T(8,128)S(1)}, f32[32,128]{1,0:T(8,128)S(1)}, u32[]{:S(2)}, u32[]{:S(2)}) collective-permute-start(f32[32,128]{1,0:T(8,128)S(1)} %get-tuple-element.28), channel_id=1, source_target_pairs={{0,7},{1,2},{2,1},{3,4},{4,3},{5,6},{6,5},{7,0},{8,15},{9,10},{10,... | collective-permute-start | bytes 49160 | tf_op jit(solution)/shard_map/ppermute | solution.py:267
  44.8 2.9 %collective-permute-start.10 = (f32[32,128]{1,0:T(8,128)S(1)}, f32[32,128]{1,0:T(8,128)S(1)}, u32[]{:S(2)}, u32[]{:S(2)}) collective-permute-start(f32[32,128]{1,0:T(8,128)S(1)} %get-tuple-element.28), channel_id=1, source_target_pairs={{0,1},{1,0},{2,3},{3,2},{4,5},{5,4},{6,7},{7,6},{8,9},{9,8},{10,11... | collective-permute-start | bytes 49160 | tf_op jit(solution)/shard_map/ppermute | solution.py:266

commit v4 on v3

--- a/solution.py
+++ b/solution.py
@@ -17,6 +17,7 @@
 ROWS = 8
 PAD = 8
 PARAMS = pltpu.CompilerParams(vmem_limit_bytes=40 * 1024 * 1024)
+FULL = pltpu.CompilerParams(vmem_limit_bytes=62 * 1024 * 1024)
 
 
 def lane_ids(rows):
@@ -65,36 +66,36 @@
     return unfold(jnp.where(odd, before, after), width)
 
 
-def pack_kernel(d_hbm, v_hbm, x1, x2, y1, y2, zm, d_ref, v_ref, sems):
+def pack_x_kernel(d_hbm, v_hbm, x1, x2, sems):
+    nx = d_hbm.shape[0]
+    (even, _, _), _, _ = edge_flags()
+    one = jnp.where(even, nx - 1, 0)
+    copies = []
+    for f, src in enumerate((d_hbm, v_hbm)):
+        copies.append(pltpu.make_async_copy(src.at[one], x1.at[f], sems.at[f, 0]))
+        copies.append(pltpu.make_async_copy(src.at[nx - 1 - one], x2.at[f], sems.at[f, 1]))
+    for copy in copies:
+        copy.start()
+    for copy in copies:
+        copy.wait()
+
+
+def pack_yz_kernel(d_ref, v_ref, y1, y2, zm):
     nx, ny, nz = d_ref.shape
-    half = nx // 2
-    copies = []
-    for f, (src, dst) in enumerate(((d_hbm, d_ref), (v_hbm, v_ref))):
-        for h in range(2):
-            part = pl.ds(h * half, half)
-            copy = pltpu.make_async_copy(src.at[part], dst.at[part], sems.at[f, h])
-            copy.start()
-            copies.append(copy)
-    (xe, _, _), (ye, _, _), _ = edge_flags()
+    _, (even, _, _), _ = edge_flags()
     lanes = lane_ids(ny)
-    edge = lanes == 0
-    pair = lanes // 2
     packed = jnp.zeros((ny, LANES), jnp.float32)
     for f, ref in enumerate((d_ref, v_ref)):
-        for h in range(2):
-            copies[2 * f + h].wait()
-            for x in range(h * half, (h + 1) * half):
-                top, bottom = ref[x, ny - 1 : ny, :], ref[x, 0:1, :]
-                y1[f, x : x + 1, :] = jnp.where(ye, top, bottom)
-                y2[f, x : x + 1, :] = jnp.where(ye, bottom, top)
-                plane = ref[x]
-                slot = f * nx + x
-                up = pltpu.roll(plane, (2 * slot + 2) % LANES, 1)
-                down = pltpu.roll(plane, 2 * slot, 1) if slot else plane
-                odd = lanes == 2 * slot + 1
-                packed = jnp.where(odd, up, jnp.where(lanes == 2 * slot, down, packed))
-        x1[f] = jnp.where(xe, ref[nx - 1], ref[0])
-        x2[f] = jnp.where(xe, ref[0], ref[nx - 1])
+        for x in range(nx):
+            top, bottom = ref[x, ny - 1 : ny, :], ref[x, 0:1, :]
+            y1[f, x : x + 1, :] = jnp.where(even, top, bottom)
+            y2[f, x : x + 1, :] = jnp.where(even, bottom, top)
+            plane = ref[x]
+            slot = f * nx + x
+            up = pltpu.roll(plane, (2 * slot + 2) % LANES, 1)
+            down = pltpu.roll(plane, 2 * slot, 1) if slot else plane
+            odd = lanes == 2 * slot + 1
+            packed = jnp.where(odd, up, jnp.where(lanes == 2 * slot, down, packed))
     zm[...] = fold(packed, 4 * nx)
 
 
@@ -282,13 +283,16 @@
     scratch = lambda *shape: pltpu.VMEM(shape, jnp.float32)
     tall = ny + 2 * PAD
 
-    x1, x2, y1, y2, zm = pl.pallas_call(
-        pack_kernel,
-        out_shape=faces,
+    x1, x2 = pl.pallas_call(
+        pack_x_kernel,
+        out_shape=faces[:2],
         in_specs=[pl.BlockSpec(memory_space=pl.ANY)] * 2,
-        out_specs=[vmem] * len(faces),
-        scratch_shapes=[scratch(nx, ny, nz), scratch(nx, ny, nz), pltpu.SemaphoreType.DMA((2, 2))],
-        compiler_params=PARAMS,
+        out_specs=[vmem] * 2,
+        scratch_shapes=[pltpu.SemaphoreType.DMA((2, 2))],
+        compiler_params=FULL,
+    )(sdf, direction)
+    y1, y2, zm = pl.pallas_call(
+        pack_yz_kernel, out_shape=faces[2:], in_specs=[vmem] * 2, out_specs=[vmem] * 3, compiler_params=PARAMS
     )(sdf, direction)
     halos = exchange((x1, y1, zm), (x2, y2, zm))
     gp, hp, x1, x2, y1, y2, zm, sums = pl.pallas_call(

time: 49.3 us -> 48.4 us (0.982)
  local copies, waits for them, and re-layouts: 2.1 us -> 0.02 us
  Pallas kernels: 7.79 us -> 9.02 us
    unnamed x12 -> x10, local copies, waits for them, and re-layouts: 2.1 us -> 0.02 us
    pallas_call x1 -> x2, Pallas kernels: 0.98 us -> 2.22 us  [the longest x1 1.59 us: body(): pl.pallas_call(pack_x_kernel, out_shape=faces[:2], in_specs=[pl.BlockSpec...]
  transfers between devices with their start and end apart: 13 -> 13, of which waited for: 4 -> 4; matrix products, arithmetic and copies ran while one was open for 0% -> 0% of each run, Pallas kernels for 0% -> 1%
where the time goes in v4:
time: 48.4 us; the launch traced here: 48.3 us
  starting transfers between devices  32.7 us (68%)
  Pallas kernels  9.02 us (19%)
  waiting for transfers between devices  5.77 us (12%)
  between operations  0.71 us (1%)
    ppermute x6, starting transfers between devices, exchange(): got.append(lax.ppermute(two, axis, outer))  16 us
    ppermute x6, starting transfers between devices, exchange(): got.append(lax.ppermute(one, axis, inner))  8.6 us
    all_to_all x1, starting transfers between devices, body(): all_sums = lax.all_to_all(sums, AXES, 0, 0, tiled=True)  8.15 us
    pallas_call x1, Pallas kernels, body(): pl.pallas_call(main_kernel, out_shape=[f32(nx + 1, ny, nz)] * 2 + faces +...  5.47 us
    ppermute x6, waiting for transfers between devices, exchange(): got.append(lax.ppermute(two, axis, outer))  4.01 us
    ppermute x6, waiting for transfers between devices, exchange(): got.append(lax.ppermute(one, axis, inner))  1.76 us
    pallas_call x1, Pallas kernels, body(): pl.pallas_call(pack_x_kernel, out_shape=faces[:2], in_specs=[pl.BlockSpec...  1.59 us
    pallas_call x1, Pallas kernels, body(): pl.pallas_call(lambda *refs: final_kernel(count, *refs), out_shape=[f32(n...  1.32 us
  transfers between devices with their start and end apart: 13, of which 4 were waited for; matrix products, arithmetic and copies ran while one was open for 0% of the time, Pallas kernels for 1%

profile of v4, /device:TPU:1, one launch (start us, length us, event | category | flops | bytes accessed | tf_op | source)
XLA Modules:
  0.0 48.3 jit_solution(14161082178149966251)
XLA Ops:
  0.6 0.0 copy-start
  0.6 0.0 copy-start.1
  0.6 1.6 %shard_map.76 = (f32[2,64,128]{2,1,0:T(8,128)}, f32[2,64,128]{2,1,0:T(8,128)}) custom-call(f32[16,64,128]{2,1,0:T(8,128)} %d_ref.3, f32[16,64,128]{2,1,0:T(8,128)} %refs_1_.1), custom_call_target="tpu_custom_call" | custom-call | tf_op jit(solution)/shard_map/pallas_call | solution.py:286
  2.2 3.3 %collective-permute-start = (f32[2,64,128]{2,1,0:T(8,128)}, f32[2,64,128]{2,1,0:T(8,128)S(1)}, u32[]{:S(2)}, u32[]{:S(2)}) collective-permute-start(f32[2,64,128]{2,1,0:T(8,128)} %get-tuple-element.16), channel_id=1, source_target_pairs={{0,64},{64,0},{128,192},{192,128},{1,65},{65,1},{129,193},{193,129... | collective-permute-start | bytes 196616 | tf_op jit(solution)/shard_map/ppermute | solution.py:267
  5.6 0.0 copy-start.2
  5.6 0.0 copy-start.3
  5.6 1.0 %collective-permute-start.1 = (f32[2,64,128]{2,1,0:T(8,128)}, f32[2,64,128]{2,1,0:T(8,128)S(1)}, u32[]{:S(2)}, u32[]{:S(2)}) collective-permute-start(f32[2,64,128]{2,1,0:T(8,128)} %get-tuple-element.17), channel_id=1, source_target_pairs={{0,192},{64,128},{128,64},{192,0},{1,193},{65,129},{129,65},{193,1... | collective-permute-start | bytes 196616 | tf_op jit(solution)/shard_map/ppermute | solution.py:268
  6.6 0.0 copy-done
  6.6 0.0 copy-done.1
  6.6 0.6 %shard_map.77 = (f32[2,16,128]{2,1,0:T(8,128)S(1)}, f32[2,16,128]{2,1,0:T(8,128)S(1)}, f32[32,128]{1,0:T(8,128)S(1)}) custom-call(f32[16,64,128]{2,1,0:T(8,128)S(1)} %copy-done.1, f32[16,64,128]{2,1,0:T(8,128)S(1)} %copy-done), custom_call_target="tpu_custom_call" | custom-call | tf_op jit(solution)/shard_map/pallas_call | solution.py:294
  7.3 1.7 %collective-permute-start.2 = (f32[2,16,128]{2,1,0:T(8,128)S(1)}, f32[2,16,128]{2,1,0:T(8,128)S(1)}, u32[]{:S(2)}, u32[]{:S(2)}) collective-permute-start(f32[2,16,128]{2,1,0:T(8,128)S(1)} %get-tuple-element.18), channel_id=1, source_target_pairs={{0,8},{8,0},{16,24},{24,16},{32,40},{40,32},{48,56},{56,48},{1,9},... | collective-permute-start | bytes 49160 | tf_op jit(solution)/shard_map/ppermute | solution.py:267
  9.0 0.0 copy-start.4
  9.0 4.7 %collective-permute-start.3 = (f32[2,16,128]{2,1,0:T(8,128)S(1)}, f32[2,16,128]{2,1,0:T(8,128)S(1)}, u32[]{:S(2)}, u32[]{:S(2)}) collective-permute-start(f32[2,16,128]{2,1,0:T(8,128)S(1)} %get-tuple-element.19), channel_id=1, source_target_pairs={{0,56},{8,16},{16,8},{24,32},{32,24},{40,48},{48,40},{56,0},{1,57}... | collective-permute-start | bytes 49160 | tf_op jit(solution)/shard_map/ppermute | solution.py:268
  13.6 2.8 %collective-permute-start.5 = (f32[32,128]{1,0:T(8,128)S(1)}, f32[32,128]{1,0:T(8,128)S(1)}, u32[]{:S(2)}, u32[]{:S(2)}) collective-permute-start(f32[32,128]{1,0:T(8,128)S(1)} %get-tuple-element.20), channel_id=1, source_target_pairs={{0,7},{1,2},{2,1},{3,4},{4,3},{5,6},{6,5},{7,0},{8,15},{9,10},{10,... | collective-permute-start | bytes 49160 | tf_op jit(solution)/shard_map/ppermute | solution.py:268
  16.4 0.0 collective-permute-done.2.y1
  16.4 0.0 collective-permute-start.4
  16.4 0.0 collective-permute-done.3.y2
  16.4 1.9 %collective-permute-done.5.z2 = f32[32,128]{1,0:T(8,128)S(1)} collective-permute-done((f32[32,128]{1,0:T(8,128)S(1)}, f32[32,128]{1,0:T(8,128)S(1)}, u32[]{:S(2)}, u32[]{:S(2)}) %collective-permute-start.5) | collective-permute-done | bytes 16416 | tf_op jit(solution)/shard_map/ppermute | solution.py:268
  18.3 1.0 %collective-permute-done.4.z1 = f32[32,128]{1,0:T(8,128)S(1)} collective-permute-done((f32[32,128]{1,0:T(8,128)S(1)}, f32[32,128]{1,0:T(8,128)S(1)}, u32[]{:S(2)}, u32[]{:S(2)}) %collective-permute-start.4) | collective-permute-done | bytes 16416 | tf_op jit(solution)/shard_map/ppermute | solution.py:267
  19.3 0.0 collective-permute-done.x1
  19.3 0.0 collective-permute-done.1.x2
  19.3 0.0 copy-done.2
  19.3 0.0 copy-done.3
  19.3 0.0 copy-done.4
  19.3 5.5 %shard_map.78 = (f32[17,64,128]{2,1,0:T(8,128)S(1)}, f32[17,64,128]{2,1,0:T(8,128)S(1)}, f32[2,64,128]{2,1,0:T(8,128)S(1)}, f32[2,64,128]{2,1,0:T(8,128)S(1)}, f...) custom-call(f32[9]{0:T(128)S(1)} %copy-done.4, ...), custom_call_target="tpu_custom_call" | custom-call | tf_op jit(solution)/shard_map/pallas_call | solution.py:298
  24.8 8.2 %all-to-all-start = ((f32[256,1,128]{2,1,0:T(1,128)}), f32[256,1,128]{2,1,0:T(1,128)S(1)}, u32[]{:S(2)}, u32[]{:S(2)}) async-start(f32[256,1,128]{2,1,0:T(1,128)} %bitcast.1), calls=%async_computation | async-start | bytes 262144 | tf_op jit(solution)/shard_map/all_to_all | solution.py:311
  33.0 2.2 %collective-permute-start.6 = (f32[2,64,128]{2,1,0:T(8,128)S(1)}, f32[2,64,128]{2,1,0:T(8,128)S(1)}, u32[]{:S(2)}, u32[]{:S(2)}) collective-permute-start(f32[2,64,128]{2,1,0:T(8,128)S(1)} %get-tuple-element.24), channel_id=1, source_target_pairs={{0,64},{64,0},{128,192},{192,128},{1,65},{65,1},{129,193},{193,129... | collective-permute-start | bytes 196616 | tf_op jit(solution)/shard_map/ppermute | solution.py:267
  35.2 1.2 %collective-permute-start.7 = (f32[2,64,128]{2,1,0:T(8,128)S(1)}, f32[2,64,128]{2,1,0:T(8,128)S(1)}, u32[]{:S(2)}, u32[]{:S(2)}) collective-permute-start(f32[2,64,128]{2,1,0:T(8,128)S(1)} %get-tuple-element.25), channel_id=1, source_target_pairs={{0,192},{64,128},{128,64},{192,0},{1,193},{65,129},{129,65},{193,1... | collective-permute-start | bytes 196616 | tf_op jit(solution)/shard_map/ppermute | solution.py:268
  36.3 1.3 %collective-permute-start.8 = (f32[2,16,128]{2,1,0:T(8,128)S(1)}, f32[2,16,128]{2,1,0:T(8,128)S(1)}, u32[]{:S(2)}, u32[]{:S(2)}) collective-permute-start(f32[2,16,128]{2,1,0:T(8,128)S(1)} %get-tuple-element.26), channel_id=1, source_target_pairs={{0,8},{8,0},{16,24},{24,16},{32,40},{40,32},{48,56},{56,48},{1,9},... | collective-permute-start | bytes 49160 | tf_op jit(solution)/shard_map/ppermute | solution.py:267
  37.7 3.7 %collective-permute-start.9 = (f32[2,16,128]{2,1,0:T(8,128)S(1)}, f32[2,16,128]{2,1,0:T(8,128)S(1)}, u32[]{:S(2)}, u32[]{:S(2)}) collective-permute-start(f32[2,16,128]{2,1,0:T(8,128)S(1)} %get-tuple-element.27), channel_id=1, source_target_pairs={{0,56},{8,16},{16,8},{24,32},{32,24},{40,48},{48,40},{56,0},{1,57}... | collective-permute-start | bytes 49160 | tf_op jit(solution)/shard_map/ppermute | solution.py:268
  41.4 2.6 %collective-permute-start.11 = (f32[32,128]{1,0:T(8,128)S(1)}, f32[32,128]{1,0:T(8,128)S(1)}, u32[]{:S(2)}, u32[]{:S(2)}) collective-permute-start(f32[32,128]{1,0:T(8,128)S(1)} %get-tuple-element.28), channel_id=1, source_target_pairs={{0,7},{1,2},{2,1},{3,4},{4,3},{5,6},{6,5},{7,0},{8,15},{9,10},{10,... | collective-permute-start | bytes 49160 | tf_op jit(solution)/shard_map/ppermute | solution.py:268
  44.0 0.0 collective-permute-done.8.refs_6_
  44.0 0.0 collective-permute-start.10
  44.0 0.0 collective-permute-done.9.refs_7_
  44.0 2.1 %collective-permute-done.11.refs_9_ = f32[32,128]{1,0:T(8,128)S(1)} collective-permute-done((f32[32,128]{1,0:T(8,128)S(1)}, f32[32,128]{1,0:T(8,128)S(1)}, u32[]{:S(2)}, u32[]{:S(2)}) %collective-permute-start.11) | collective-permute-done | bytes 16416 | tf_op jit(solution)/shard_map/ppermute | solution.py:268
  46.1 0.8 %collective-permute-done.10.refs_8_ = f32[32,128]{1,0:T(8,128)S(1)} collective-permute-done((f32[32,128]{1,0:T(8,128)S(1)}, f32[32,128]{1,0:T(8,128)S(1)}, u32[]{:S(2)}, u32[]{:S(2)}) %collective-permute-start.10) | collective-permute-done | bytes 16416 | tf_op jit(solution)/shard_map/ppermute | solution.py:267
  46.9 0.0 collective-permute-done.6.refs_4_
  46.9 0.0 collective-permute-done.7.refs_5_
  46.9 0.0 all-to-all-done
  46.9 1.3 %shard_map.79 = (f32[16,64,128]{2,1,0:T(8,128)}, f32[16,64,128]{2,1,0:T(8,128)}, f32[9]{0:T(128)}) custom-call(f32[256,128]{1,0:T(8,128)S(1)} %bitcast.4, f32[16,64,128]{2,1,0:T(8,128)S(1)} %copy-done, f32[17,64,128]{2,1,0:T(8,128)S(1)} %get-tuple-element.22.refs_2_, f32[17,64,128]{2,1,0:T(8,128)S(1)} %get-tuple-element.23.refs_3_, ...), custom_call_target="tpu_custom_call" | custom-call | tf_op jit(solution)/shard_map/pallas_call | solution.py:312
Async XLA Ops:
  0.6 6.0 %copy-start = (f32[16,64,128]{2,1,0:T(8,128)S(1)}, f32[16,64,128]{2,1,0:T(8,128)}, u32[]{:S(2)}) copy-start(f32[16,64,128]{2,1,0:T(8,128)} %refs_1_.1) | copy-start | bytes 1572868
  0.6 6.0 %copy-start.1 = (f32[16,64,128]{2,1,0:T(8,128)S(1)}, f32[16,64,128]{2,1,0:T(8,128)}, u32[]{:S(2)}) copy-start(f32[16,64,128]{2,1,0:T(8,128)} %d_ref.3) | copy-start | bytes 1572868
  2.2 17.0 %collective-permute-start = (f32[2,64,128]{2,1,0:T(8,128)}, f32[2,64,128]{2,1,0:T(8,128)S(1)}, u32[]{:S(2)}, u32[]{:S(2)}) collective-permute-start(f32[2,64,128]{2,1,0:T(8,128)} %get-tuple-element.16), channel_id=1, source_target_pairs={{0,64},{64,0},{128,192},{192,128},{1,65},{65,1},{129,193},{193,129... | collective-permute-start | bytes 196616 | tf_op jit(solution)/shard_map/ppermute | solution.py:267
  5.6 13.7 %copy-start.2 = (f32[16,64,128]{2,1,0:T(8,128)S(1)}, f32[16,64,128]{2,1,0:T(8,128)}, u32[]{:S(2)}) copy-start(f32[16,64,128]{2,1,0:T(8,128)} %a_ref.1) | copy-start | bytes 1572868
  5.6 13.7 %copy-start.3 = (f32[16,64,128]{2,1,0:T(8,128)S(1)}, f32[16,64,128]{2,1,0:T(8,128)}, u32[]{:S(2)}) copy-start(f32[16,64,128]{2,1,0:T(8,128)} %i_ref.1) | copy-start | bytes 1572868
  5.6 13.7 %collective-permute-start.1 = (f32[2,64,128]{2,1,0:T(8,128)}, f32[2,64,128]{2,1,0:T(8,128)S(1)}, u32[]{:S(2)}, u32[]{:S(2)}) collective-permute-start(f32[2,64,128]{2,1,0:T(8,128)} %get-tuple-element.17), channel_id=1, source_target_pairs={{0,192},{64,128},{128,64},{192,0},{1,193},{65,129},{129,65},{193,1... | collective-permute-start | bytes 196616 | tf_op jit(solution)/shard_map/ppermute | solution.py:268
  7.3 9.1 %collective-permute-start.2 = (f32[2,16,128]{2,1,0:T(8,128)S(1)}, f32[2,16,128]{2,1,0:T(8,128)S(1)}, u32[]{:S(2)}, u32[]{:S(2)}) collective-permute-start(f32[2,16,128]{2,1,0:T(8,128)S(1)} %get-tuple-element.18), channel_id=1, source_target_pairs={{0,8},{8,0},{16,24},{24,16},{32,40},{40,32},{48,56},{56,48},{1,9},... | collective-permute-start | bytes 49160 | tf_op jit(solution)/shard_map/ppermute | solution.py:267
  9.0 10.3 %copy-start.4 = (f32[9]{0:T(128)S(1)}, f32[9]{0:T(128)}, u32[]{:S(2)}) copy-start(f32[9]{0:T(128)} %light.1) | copy-start | bytes 112
  9.0 7.4 %collective-permute-start.3 = (f32[2,16,128]{2,1,0:T(8,128)S(1)}, f32[2,16,128]{2,1,0:T(8,128)S(1)}, u32[]{:S(2)}, u32[]{:S(2)}) collective-permute-start(f32[2,16,128]{2,1,0:T(8,128)S(1)} %get-tuple-element.19), channel_id=1, source_target_pairs={{0,56},{8,16},{16,8},{24,32},{32,24},{40,48},{48,40},{56,0},{1,57}... | collective-permute-start | bytes 49160 | tf_op jit(solution)/shard_map/ppermute | solution.py:268
  13.6 4.7 %collective-permute-start.5 = (f32[32,128]{1,0:T(8,128)S(1)}, f32[32,128]{1,0:T(8,128)S(1)}, u32[]{:S(2)}, u32[]{:S(2)}) collective-permute-start(f32[32,128]{1,0:T(8,128)S(1)} %get-tuple-element.20), channel_id=1, source_target_pairs={{0,7},{1,2},{2,1},{3,4},{4,3},{5,6},{6,5},{7,0},{8,15},{9,10},{10,... | collective-permute-start | bytes 49160 | tf_op jit(solution)/shard_map/ppermute | solution.py:268
  16.4 2.9 %collective-permute-start.4 = (f32[32,128]{1,0:T(8,128)S(1)}, f32[32,128]{1,0:T(8,128)S(1)}, u32[]{:S(2)}, u32[]{:S(2)}) collective-permute-start(f32[32,128]{1,0:T(8,128)S(1)} %get-tuple-element.20), channel_id=1, source_target_pairs={{0,1},{1,0},{2,3},{3,2},{4,5},{5,4},{6,7},{7,6},{8,9},{9,8},{10,11... | collective-permute-start | bytes 49160 | tf_op jit(solution)/shard_map/ppermute | solution.py:267
  24.8 22.1 %all-to-all-start = ((f32[256,1,128]{2,1,0:T(1,128)}), f32[256,1,128]{2,1,0:T(1,128)S(1)}, u32[]{:S(2)}, u32[]{:S(2)}) async-start(f32[256,1,128]{2,1,0:T(1,128)} %bitcast.1), calls=%async_computation | async-start | bytes 262144 | tf_op jit(solution)/shard_map/all_to_all | solution.py:311
  33.0 14.0 %collective-permute-start.6 = (f32[2,64,128]{2,1,0:T(8,128)S(1)}, f32[2,64,128]{2,1,0:T(8,128)S(1)}, u32[]{:S(2)}, u32[]{:S(2)}) collective-permute-start(f32[2,64,128]{2,1,0:T(8,128)S(1)} %get-tuple-element.24), channel_id=1, source_target_pairs={{0,64},{64,0},{128,192},{192,128},{1,65},{65,1},{129,193},{193,129... | collective-permute-start | bytes 196616 | tf_op jit(solution)/shard_map/ppermute | solution.py:267
  35.2 11.7 %collective-permute-start.7 = (f32[2,64,128]{2,1,0:T(8,128)S(1)}, f32[2,64,128]{2,1,0:T(8,128)S(1)}, u32[]{:S(2)}, u32[]{:S(2)}) collective-permute-start(f32[2,64,128]{2,1,0:T(8,128)S(1)} %get-tuple-element.25), channel_id=1, source_target_pairs={{0,192},{64,128},{128,64},{192,0},{1,193},{65,129},{129,65},{193,1... | collective-permute-start | bytes 196616 | tf_op jit(solution)/shard_map/ppermute | solution.py:268
  36.3 7.7 %collective-permute-start.8 = (f32[2,16,128]{2,1,0:T(8,128)S(1)}, f32[2,16,128]{2,1,0:T(8,128)S(1)}, u32[]{:S(2)}, u32[]{:S(2)}) collective-permute-start(f32[2,16,128]{2,1,0:T(8,128)S(1)} %get-tuple-element.26), channel_id=1, source_target_pairs={{0,8},{8,0},{16,24},{24,16},{32,40},{40,32},{48,56},{56,48},{1,9},... | collective-permute-start | bytes 49160 | tf_op jit(solution)/shard_map/ppermute | solution.py:267
  37.7 6.4 %collective-permute-start.9 = (f32[2,16,128]{2,1,0:T(8,128)S(1)}, f32[2,16,128]{2,1,0:T(8,128)S(1)}, u32[]{:S(2)}, u32[]{:S(2)}) collective-permute-start(f32[2,16,128]{2,1,0:T(8,128)S(1)} %get-tuple-element.27), channel_id=1, source_target_pairs={{0,56},{8,16},{16,8},{24,32},{32,24},{40,48},{48,40},{56,0},{1,57}... | collective-permute-start | bytes 49160 | tf_op jit(solution)/shard_map/ppermute | solution.py:268
  41.4 4.7 %collective-permute-start.11 = (f32[32,128]{1,0:T(8,128)S(1)}, f32[32,128]{1,0:T(8,128)S(1)}, u32[]{:S(2)}, u32[]{:S(2)}) collective-permute-start(f32[32,128]{1,0:T(8,128)S(1)} %get-tuple-element.28), channel_id=1, source_target_pairs={{0,7},{1,2},{2,1},{3,4},{4,3},{5,6},{6,5},{7,0},{8,15},{9,10},{10,... | collective-permute-start | bytes 49160 | tf_op jit(solution)/shard_map/ppermute | solution.py:268
  44.0 2.9 %collective-permute-start.10 = (f32[32,128]{1,0:T(8,128)S(1)}, f32[32,128]{1,0:T(8,128)S(1)}, u32[]{:S(2)}, u32[]{:S(2)}) collective-permute-start(f32[32,128]{1,0:T(8,128)S(1)} %get-tuple-element.28), channel_id=1, source_target_pairs={{0,1},{1,0},{2,3},{3,2},{4,5},{5,4},{6,7},{7,6},{8,9},{9,8},{10,11... | collective-permute-start | bytes 49160 | tf_op jit(solution)/shard_map/ppermute | solution.py:267
